TPU v7x, 32 devices: a whole 2x2x4 slice. The times are simulated.
32 devices in a mesh: dp: 8 (over z, x), shard: 4 (over y, core).
Axes of the slice: x: 2, y: 2, z: 4, core: 2. Of those that a mesh axis runs over, the one named last changes fastest.
Arguments:
- inputs: bfloat16 [128, 256, 512], P(('dp', 'shard')), may hold values from -6 to 6
- lengths: int32 [128], P(('dp', 'shard')), may hold values from 1 to 250, as said below
- slot_order: int32 [128, 256], P(('dp', 'shard')), may hold values from 0 to 255, each once within a row
- ln1_gain: bfloat16 [512], P(('dp', 'shard')), may hold values from 0.099609375 to 1.8984375
- ln1_bias: bfloat16 [512], P(('dp', 'shard')), may hold values from -1.75 to 1.75
- w_qkv: bfloat16 [512, 1536], P(('dp', 'shard')), may hold values from -0.25 to 0.25
- q_bias: bfloat16 [512], P(('dp', 'shard')), may hold values from -1.75 to 1.75
- v_bias: bfloat16 [512], P(('dp', 'shard')), may hold values from -1.75 to 1.75
- w_out: bfloat16 [512, 512], P(('dp', 'shard')), may hold values from -2 to 2
- out_bias: bfloat16 [512], P(('dp', 'shard')), may hold values from -1.75 to 1.75
- ln2_gain: bfloat16 [512], P(('dp', 'shard')), may hold values from 0.099609375 to 1.8984375
- ln2_bias: bfloat16 [512], P(('dp', 'shard')), may hold values from -1.75 to 1.75
- w_up: bfloat16 [512, 2048], P(('dp', 'shard')), may hold values from -0.25 to 0.25
- up_bias: bfloat16 [2048], P(('dp', 'shard')), may hold values from -1.75 to 1.75
- w_down: bfloat16 [2048, 512], P(('dp', 'shard')), may hold values from -0.125 to 0.125
- down_bias: bfloat16 [512], P(('dp', 'shard')), may hold values from -1.75 to 1.75
- cotangent: bfloat16 [128, 256, 512], P(('dp', 'shard')), may hold values from -6 to 6
Outputs:
- output: bfloat16 [128, 256, 512], P(('dp', 'shard'))
- input_grad: float32 [128, 256, 512], P(('dp', 'shard'))
- ln1_gain_grad: float32 [512], P(('dp', 'shard'))
- ln1_bias_grad: float32 [512], P(('dp', 'shard'))
- w_qkv_grad: float32 [512, 1536], P(('dp', 'shard'))
- q_bias_grad: float32 [512], P(('dp', 'shard'))
- v_bias_grad: float32 [512], P(('dp', 'shard'))
- w_out_grad: float32 [512, 512], P(('dp', 'shard'))
- out_bias_grad: float32 [512], P(('dp', 'shard'))
- ln2_gain_grad: float32 [512], P(('dp', 'shard'))
- ln2_bias_grad: float32 [512], P(('dp', 'shard'))
- w_up_grad: float32 [512, 2048], P(('dp', 'shard'))
- up_bias_grad: float32 [2048], P(('dp', 'shard'))
- w_down_grad: float32 [2048, 512], P(('dp', 'shard'))
- down_bias_grad: float32 [512], P(('dp', 'shard'))
Inputs may be any that keep to these rules, and one draw needn't show every extreme that they name: `lengths`: some row has exactly 250 valid slots and some row exactly 1. `slot_order`: each row is an ordering of its 256 slots.
All inputs are finite; a program needn't handle non-finite values.
Results may differ from a plain program's by a relative error of at most 0.012.
Values may be sent and summed in bfloat16 or wider, within the bound.
A program may use at most 128 MiB of HBM per device.

v0:
```python
import jax
import jax.numpy as jnp
from jax import lax
from jax.sharding import PartitionSpec as P

HEADS = 8
HEAD_DIM = 64


epsilon = 1e-05
masked_value = -1e30


def layer_norm(values, gain, shift):
    centre = jnp.mean(values, axis=-1, keepdims=True)
    centred = values - centre
    spread = jnp.mean(centred * centred, axis=-1, keepdims=True)
    return centred * lax.rsqrt(spread + epsilon) * gain + shift


def allowed_pairs(lengths, slot_order):
    slot_count = slot_order.shape[-1]
    place = jnp.arange(slot_count, dtype=jnp.int32)
    valid = place[None, :] < lengths[:, None]
    earlier = slot_order[:, None, :] <= slot_order[:, :, None]
    same = place[:, None] == place[None, :]
    return valid[:, None, :] & earlier | same[None]


def masked_scores(queries, keys_proj, lengths, slot_order):
    scores = jnp.einsum("rqhd,rkhd->rhqk", queries, keys_proj, preferred_element_type=jnp.float32)
    scores = scores * HEAD_DIM ** (-0.5)
    allowed = allowed_pairs(lengths, slot_order)[:, None]
    return jnp.where(allowed, scores, masked_value)


def attend_block(member):
    queries, keys_proj, values_proj, lengths, slot_order = member
    scores = masked_scores(queries, keys_proj, lengths, slot_order)
    row_max = jnp.max(scores, axis=-1, keepdims=True)
    weights_exp = jnp.exp(scores - row_max)
    row_total = jnp.sum(weights_exp, axis=-1, keepdims=True)
    probs = (weights_exp / row_total).astype(jnp.bfloat16)
    mixed = jnp.einsum("rhqk,rkhd->rqhd", probs, values_proj, preferred_element_type=jnp.float32)
    return (mixed.astype(jnp.bfloat16), (row_max + jnp.log(row_total))[..., 0])


def attend_back(member):
    queries, keys_proj, values_proj, grad_mixed, logsum, lengths, slot_order = member
    scores = masked_scores(queries, keys_proj, lengths, slot_order)
    probs = jnp.exp(scores - logsum[..., None])
    low_probs = probs.astype(jnp.bfloat16)
    grad_values = jnp.einsum(
        "rhqk,rqhd->rkhd", low_probs, grad_mixed, preferred_element_type=jnp.float32
    )
    grad_probs = jnp.einsum(
        "rqhd,rkhd->rhqk", grad_mixed, values_proj, preferred_element_type=jnp.float32
    )
    row_delta = jnp.sum(probs * grad_probs, axis=-1, keepdims=True)
    grad_scores = (probs * (grad_probs - row_delta)).astype(jnp.bfloat16)
    score_scale = HEAD_DIM ** (-0.5)
    grad_queries = (
        jnp.einsum("rhqk,rkhd->rqhd", grad_scores, keys_proj, preferred_element_type=jnp.float32)
        * score_scale
    )
    grad_keys = (
        jnp.einsum("rhqk,rqhd->rkhd", grad_scores, queries, preferred_element_type=jnp.float32)
        * score_scale
    )
    return (
        grad_queries.astype(jnp.bfloat16),
        grad_keys.astype(jnp.bfloat16),
        grad_values.astype(jnp.bfloat16),
    )


def shards(
    inputs,
    lengths,
    slot_order,
    ln1_gain,
    ln1_bias,
    w_qkv,
    q_bias,
    v_bias,
    w_out,
    out_bias,
    ln2_gain,
    ln2_bias,
    w_up,
    up_bias,
    w_down,
    down_bias,
    cotangent,
):
    row_count, slot_count, model_width = inputs.shape
    tokens = row_count * slot_count
    flat_rows = inputs.reshape(tokens, model_width).astype(jnp.float32)
    attn_full = (
        lax.all_gather(ln1_gain, ("dp", "shard"), axis=0, tiled=True),
        lax.all_gather(ln1_bias, ("dp", "shard"), axis=0, tiled=True),
        lax.all_gather(w_qkv, ("dp", "shard"), axis=0, tiled=True),
        lax.all_gather(q_bias, ("dp", "shard"), axis=0, tiled=True),
        lax.all_gather(v_bias, ("dp", "shard"), axis=0, tiled=True),
        lax.all_gather(w_out, ("dp", "shard"), axis=0, tiled=True),
        lax.all_gather(out_bias, ("dp", "shard"), axis=0, tiled=True),
    )
    gain_one = attn_full[0].astype(jnp.float32)
    shift_one = attn_full[1].astype(jnp.float32)
    qkv_full = attn_full[2]
    out_full = attn_full[5]
    normed = layer_norm(flat_rows, gain_one, shift_one).astype(jnp.bfloat16)
    projected = jnp.dot(normed, qkv_full, preferred_element_type=jnp.float32)
    queries = (projected[:, :model_width] + attn_full[3].astype(jnp.float32)).astype(jnp.bfloat16)
    keys_proj = projected[:, model_width : 2 * model_width].astype(jnp.bfloat16)
    values_proj = (projected[:, 2 * model_width :] + attn_full[4].astype(jnp.float32)).astype(
        jnp.bfloat16
    )
    block_shape = (row_count // 2, 2, slot_count, HEADS, HEAD_DIM)
    query_blocks = queries.reshape(block_shape)
    key_blocks = keys_proj.reshape(block_shape)
    value_blocks = values_proj.reshape(block_shape)
    length_blocks = lengths.reshape(row_count // 2, 2)
    order_blocks = slot_order.reshape(row_count // 2, 2, slot_count)
    mixed_blocks, logsum = lax.map(
        attend_block, (query_blocks, key_blocks, value_blocks, length_blocks, order_blocks)
    )
    mixed = mixed_blocks.reshape(tokens, model_width)
    attended = jnp.dot(mixed, out_full, preferred_element_type=jnp.float32) + attn_full[6].astype(
        jnp.float32
    )
    middle = flat_rows + attended
    mlp_full = (
        lax.all_gather(ln2_gain, ("dp", "shard"), axis=0, tiled=True),
        lax.all_gather(ln2_bias, ("dp", "shard"), axis=0, tiled=True),
        lax.all_gather(w_up, ("dp", "shard"), axis=0, tiled=True),
        lax.all_gather(up_bias, ("dp", "shard"), axis=0, tiled=True),
        lax.all_gather(w_down, ("dp", "shard"), axis=0, tiled=True),
        lax.all_gather(down_bias, ("dp", "shard"), axis=0, tiled=True),
    )
    gain_two = mlp_full[0].astype(jnp.float32)
    shift_two = mlp_full[1].astype(jnp.float32)
    normed_two = layer_norm(middle, gain_two, shift_two).astype(jnp.bfloat16)
    up_proj = jnp.dot(normed_two, mlp_full[2], preferred_element_type=jnp.float32) + mlp_full[
        3
    ].astype(jnp.float32)
    activated = jax.nn.gelu(up_proj).astype(jnp.bfloat16)
    down_proj = jnp.dot(activated, mlp_full[4], preferred_element_type=jnp.float32) + mlp_full[
        5
    ].astype(jnp.float32)
    output = (middle + down_proj).astype(jnp.bfloat16).reshape(row_count, slot_count, model_width)
    grad_out = cotangent.reshape(tokens, model_width).astype(jnp.float32)
    mlp_back = (
        lax.all_gather(ln2_gain, ("dp", "shard"), axis=0, tiled=True),
        lax.all_gather(ln2_bias, ("dp", "shard"), axis=0, tiled=True),
        lax.all_gather(w_up, ("dp", "shard"), axis=0, tiled=True),
        lax.all_gather(up_bias, ("dp", "shard"), axis=0, tiled=True),
        lax.all_gather(w_down, ("dp", "shard"), axis=0, tiled=True),
        lax.all_gather(down_bias, ("dp", "shard"), axis=0, tiled=True),
    )
    grad_down = grad_out.astype(jnp.bfloat16)
    down_bias_grad = jnp.sum(grad_down.astype(jnp.float32), axis=0)
    w_down_grad = jnp.einsum("tf,to->fo", activated, grad_down, preferred_element_type=jnp.float32)
    grad_act = jnp.einsum("to,fo->tf", grad_down, mlp_back[4], preferred_element_type=jnp.float32)
    gelu_value, gelu_pull = jax.vjp(jax.nn.gelu, up_proj)
    grad_pre = gelu_pull(grad_act)[0].astype(jnp.bfloat16)
    up_bias_grad = jnp.sum(grad_pre.astype(jnp.float32), axis=0)
    w_up_grad = jnp.einsum("td,tf->df", normed_two, grad_pre, preferred_element_type=jnp.float32)
    grad_normed_two = jnp.einsum(
        "tf,df->td", grad_pre, mlp_back[2], preferred_element_type=jnp.float32
    )
    norm_value, norm_pull = jax.vjp(
        layer_norm, middle, mlp_back[0].astype(jnp.float32), mlp_back[1].astype(jnp.float32)
    )
    grad_middle_norm, ln2_gain_grad, ln2_bias_grad = norm_pull(grad_normed_two)
    grad_middle = grad_out + grad_middle_norm
    mlp_owned = (
        lax.psum_scatter(ln2_gain_grad, ("dp", "shard"), scatter_dimension=0, tiled=True),
        lax.psum_scatter(ln2_bias_grad, ("dp", "shard"), scatter_dimension=0, tiled=True),
        lax.psum_scatter(w_up_grad, ("dp", "shard"), scatter_dimension=0, tiled=True),
        lax.psum_scatter(up_bias_grad, ("dp", "shard"), scatter_dimension=0, tiled=True),
        lax.psum_scatter(w_down_grad, ("dp", "shard"), scatter_dimension=0, tiled=True),
        lax.psum_scatter(down_bias_grad, ("dp", "shard"), scatter_dimension=0, tiled=True),
    )
    attn_back = (
        lax.all_gather(ln1_gain, ("dp", "shard"), axis=0, tiled=True),
        lax.all_gather(ln1_bias, ("dp", "shard"), axis=0, tiled=True),
        lax.all_gather(w_qkv, ("dp", "shard"), axis=0, tiled=True),
        lax.all_gather(q_bias, ("dp", "shard"), axis=0, tiled=True),
        lax.all_gather(v_bias, ("dp", "shard"), axis=0, tiled=True),
        lax.all_gather(w_out, ("dp", "shard"), axis=0, tiled=True),
        lax.all_gather(out_bias, ("dp", "shard"), axis=0, tiled=True),
    )
    grad_attended = grad_middle.astype(jnp.bfloat16)
    out_bias_grad = jnp.sum(grad_attended.astype(jnp.float32), axis=0)
    w_out_grad = jnp.einsum("ti,to->io", mixed, grad_attended, preferred_element_type=jnp.float32)
    grad_mixed = jnp.einsum(
        "to,io->ti", grad_attended, attn_back[5], preferred_element_type=jnp.float32
    ).astype(jnp.bfloat16)
    grad_q_blocks, grad_k_blocks, grad_v_blocks = lax.map(
        attend_back,
        (
            query_blocks,
            key_blocks,
            value_blocks,
            grad_mixed.reshape(block_shape),
            logsum,
            length_blocks,
            order_blocks,
        ),
    )
    grad_queries = grad_q_blocks.reshape(tokens, model_width)
    grad_keys = grad_k_blocks.reshape(tokens, model_width)
    grad_values = grad_v_blocks.reshape(tokens, model_width)
    grad_projected = jnp.concatenate([grad_queries, grad_keys, grad_values], axis=1)
    q_bias_grad = jnp.sum(grad_queries.astype(jnp.float32), axis=0)
    v_bias_grad = jnp.sum(grad_values.astype(jnp.float32), axis=0)
    w_qkv_grad = jnp.einsum("td,tj->dj", normed, grad_projected, preferred_element_type=jnp.float32)
    grad_normed = jnp.einsum(
        "tj,dj->td", grad_projected, attn_back[2], preferred_element_type=jnp.float32
    )
    first_value, first_pull = jax.vjp(
        layer_norm, flat_rows, attn_back[0].astype(jnp.float32), attn_back[1].astype(jnp.float32)
    )
    grad_flat_norm, ln1_gain_grad, ln1_bias_grad = first_pull(grad_normed)
    input_grad = (grad_middle + grad_flat_norm).reshape(row_count, slot_count, model_width)
    attn_owned = (
        lax.psum_scatter(ln1_gain_grad, ("dp", "shard"), scatter_dimension=0, tiled=True),
        lax.psum_scatter(ln1_bias_grad, ("dp", "shard"), scatter_dimension=0, tiled=True),
        lax.psum_scatter(w_qkv_grad, ("dp", "shard"), scatter_dimension=0, tiled=True),
        lax.psum_scatter(q_bias_grad, ("dp", "shard"), scatter_dimension=0, tiled=True),
        lax.psum_scatter(v_bias_grad, ("dp", "shard"), scatter_dimension=0, tiled=True),
        lax.psum_scatter(w_out_grad, ("dp", "shard"), scatter_dimension=0, tiled=True),
        lax.psum_scatter(out_bias_grad, ("dp", "shard"), scatter_dimension=0, tiled=True),
    )
    return (
        output,
        input_grad,
        attn_owned[0],
        attn_owned[1],
        attn_owned[2],
        attn_owned[3],
        attn_owned[4],
        attn_owned[5],
        attn_owned[6],
        mlp_owned[0],
        mlp_owned[1],
        mlp_owned[2],
        mlp_owned[3],
        mlp_owned[4],
        mlp_owned[5],
    )


def solution(mesh):
    placed = (
        P(("dp", "shard"), None, None),
        P(("dp", "shard")),
        P(("dp", "shard"), None),
        P(("dp", "shard")),
        P(("dp", "shard")),
        P(("dp", "shard"), None),
        P(("dp", "shard")),
        P(("dp", "shard")),
        P(("dp", "shard"), None),
        P(("dp", "shard")),
        P(("dp", "shard")),
        P(("dp", "shard")),
        P(("dp", "shard"), None),
        P(("dp", "shard")),
        P(("dp", "shard"), None),
        P(("dp", "shard")),
        P(("dp", "shard"), None, None),
    )
    return jax.shard_map(
        shards,
        mesh=mesh,
        in_specs=placed,
        out_specs=(
            P(("dp", "shard"), None, None),
            P(("dp", "shard"), None, None),
            P(("dp", "shard")),
            P(("dp", "shard")),
            P(("dp", "shard"), None),
            P(("dp", "shard")),
            P(("dp", "shard")),
            P(("dp", "shard"), None),
            P(("dp", "shard")),
            P(("dp", "shard")),
            P(("dp", "shard")),
            P(("dp", "shard"), None),
            P(("dp", "shard")),
            P(("dp", "shard"), None),
            P(("dp", "shard")),
        ),
        check_vma=False,
    )
```

profile of v0, /device:TPU:0, one launch (start us, length us, event | category | flops | bytes accessed | tf_op | source)
XLA Modules:
  0.0 740.5 jit_solution(15819630416213874091)
XLA Ops:
  17.2 42.2 %all-reduce.19 = (bf16[512]{0:T(512)(128)(2,1)S(1)}, bf16[512]{0:T(512)(128)(2,1)S(1)}, bf16[512]{0:T(512)(128)(2,1)S(1)}, bf16[512]{0:T(512)(128)(2,1)S(1)}, bf...) all-reduce(bf16[512]{0:T(512)(128)(2,1)S(1)} %dynamic-update-slice., ...), channel_id=1, replica_groups=mesh['dp'=8,'shard'=4] {'dp','shard'}, use_global_device_ids=true, to_apply=%add.1 | all-reduce | flops 6144 | bytes 24576
  59.4 1.4 convert_reduce_fusion.1
  60.9 1.7 fusion.82
  63.3 45.0 %all_gather.50 = bf16[512,512]{1,0:T(8,128)(2,1)} all-gather(bf16[16,512]{1,0:T(8,128)(2,1)S(1)} %copy-done.32), channel_id=1, replica_groups=mesh['dp'=8,'shard'=4] {'dp','shard'}, dimensions={0}, use_global_device_ids=true | all-gather | bytes 540672 | tf_op jit(solution)/shard_map/all_gather | solution.py:105
  108.8 3.6 fusion.93
  112.4 1.2 slice.23
  113.6 1.9 fusion.70
  115.5 3.2 reshape.301
  118.8 1.9 copy.69
  120.7 3.9 reshape.302
  124.6 2.3 copy.70
  126.9 2.1 reshape.303
  129.0 2.2 copy.71
  131.2 1.5 broadcast.183.clone2
  132.7 10.0 %while.26 = (s32[]{:T(128)}, bf16[2,2,256,8,64]{2,1,0,4,3:T(2,128)(2,1)}, f32[2,2,8,256]{3,2,1,0:T(8,128)S(1)}, bf16[2,2,256,8,64]{2,4,3,1,0:T(8,128)(2,1)}, s32...) while((s32[]{:T(128)}, ...), condition=%wide.region_5.6_spmd, body=%wide.region_2.5_spmd.sunk | while | flops 281735680 | bytes 20718240 | solution.py:125
  135.2 1.2 fusion.144
  136.4 1.3 copy_dynamic-update-slice_fusion.4
  140.2 1.2 fusion.144
  141.4 1.3 copy_dynamic-update-slice_fusion.4
  142.7 2.6 reshape.273
  145.4 2.2 fusion.92
  147.6 1.3 copy-done
  149.4 9.2 %multiply_convert_fusion.1 = (bf16[1024,2048]{1,0:T(8,128)(2,1)}, f32[1024,2048]{1,0:T(8,128)}) fusion(f32[2048]{0:T(1024)S(1)} %convert_element_type.136, bf16[512,2048]{1,0:T(8,128)(2,1)} %all-gather.6.cloned.1.call-done, f32[1024,512]{1,0:T(8,128)} %copy-done, f32[512]{0:T(512)S(1)} %convert_element_type.134, f32[512]{0:T(512)S(1)} %convert_element_type.133, ...), kind=kOutput, calls=%fused_computation.88 | convolution fusion | flops 2171076608 | bytes 16797696 | tf_op jit(solution)/shard_map/dot_general | solution.py:144
  158.5 26.8 %all-gather.8.cloned.1.call-done = bf16[2048,512]{1,0:T(8,128)(2,1)} async-done(((bf16[64,512]{1,0:T(8,128)(2,1)}), bf16[2048,512]{1,0:T(8,128)(2,1)}) %all-gather.8.cloned.1.call-update) | async-done | bytes 2097168 | tf_op jit(solution)/shard_map/all_gather | solution.py:138
  185.3 10.4 %convert_reduce_fusion = (f32[2048]{0:T(1024)S(1)}, bf16[1024,2048]{1,0:T(8,128)(2,1)S(1)}) fusion(f32[1024,2048]{1,0:T(8,128)} %get-tuple-element.257, f32[2048]{0:T(1024)S(1)} %convert_element_type.136, bf16[1024,512]{1,0:T(8,128)(2,1)} %bitcast.182, bf16[2048,512]{1,0:T(8,128)(2,1)} %all-gather.8.cloned.1.call-done), kind=kOutput, calls=%fused_computation.87 | convolution fusion | flops 2195716096 | bytes 15745024 | tf_op jit(solution)/shard_map/to,fo->tf/dot_general | solution.py:164
  195.8 2.9 multiply_reduce_fusion.1
  201.3 1.7 convolution_convert_fusion
  203.1 1.8 fusion.95
  204.8 3.9 reshape.300
  208.7 3.0 copy.76
  211.8 1.5 broadcast.183.clone
  213.4 20.0 %while.27 = (s32[]{:T(128)}, bf16[2,2,256,8,64]{2,4,3,1,0:T(8,128)(2,1)}, bf16[2,2,256,8,64]{2,1,0,4,3:T(2,128)(2,1)}, bf16[2,2,256,8,64]{2,4,3,1,0:T(8,128)(2,1...) while((s32[]{:T(128)}, ...), condition=%wide.region_12.13_spmd, body=%wide.region_10.12_spmd.sunk | while | flops 688583168 | bytes 63696200 | solution.py:200
  215.5 1.4 multiply_reduce_fusion.5
  216.8 1.3 multiply_convert_fusion.3
  220.5 1.0 copy-done.13
  221.6 1.9 fusion.158
  225.3 1.4 multiply_reduce_fusion.5
  226.7 1.3 multiply_convert_fusion.3
  230.4 1.0 copy-done.13
  231.4 1.9 fusion.158
  233.4 3.4 copy.78
  236.8 1.8 reshape.277
  238.6 1.5 reshape.278
  240.2 3.4 copy.80
  243.5 2.7 reshape.279
  246.4 1.1 copy-done.18
  247.5 1.7 copy-done.23
  249.1 3.5 fusion.94
  253.0 1.3 copy-done.2
  254.3 6.7 fusion.87
  261.0 6.8 fusion.96
  268.4 1.4 convert_reduce_fusion.2
  269.9 1.9 convert_reduce_fusion.4
  271.9 4.6 fusion.89
  276.6 1.3 copy-done.10
  277.9 1.2 fusion.79
  279.1 39.0 %all-reduce.18 = (f32[512]{0:T(512)S(1)}, f32[512]{0:T(512)S(1)}, f32[512]{0:T(512)S(1)}, f32[512]{0:T(512)S(1)}, f32[512]{0:T(512)S(1)}, /*index=5*/f32[512]{0:...) all-reduce(f32[512]{0:T(512)S(1)} %get-tuple-element.181, ...), channel_id=2, replica_groups=mesh['dp'=8,'shard'=4] {'dp','shard'}, use_global_device_ids=true, to_apply=%region_16.17.clone | all-reduce | flops 6144 | bytes 49152
  323.3 4.1 add_add_fusion.2
  327.4 1.0 copy-done.38
  328.5 3.3 add_convert_fusion
  331.8 13.9 %reduce-scatter.7.cloned.1.call-done = f32[16,512]{1,0:T(8,128)} async-done(((f32[512,512]{1,0:T(8,128)}), f32[16,512]{1,0:T(8,128)}) %reduce-scatter.7.cloned.1.call-update) | async-done | bytes 32784 | tf_op jit(solution)/shard_map/reduce_scatter | solution.py:233
  345.7 104.2 %reduce-scatter.5.cloned.1.call-done = f32[16,1536]{1,0:T(8,128)} async-done(((f32[512,1536]{1,0:T(8,128)}), f32[16,1536]{1,0:T(8,128)}) %reduce-scatter.5.cloned.1.call-update) | async-done | bytes 98320 | tf_op jit(solution)/shard_map/reduce_scatter | solution.py:230
  449.9 143.2 %reduce-scatter.9.cloned.1.call-done = f32[16,2048]{1,0:T(8,128)} async-done(((f32[512,2048]{1,0:T(8,128)}), f32[16,2048]{1,0:T(8,128)}) %reduce-scatter.9.cloned.1.call-update) | async-done | bytes 131088 | tf_op jit(solution)/shard_map/reduce_scatter | solution.py:180
  593.1 140.1 %reduce-scatter.11.cloned.1.call-done = f32[64,512]{1,0:T(8,128)} async-done(((f32[2048,512]{1,0:T(8,128)}), f32[64,512]{1,0:T(8,128)}) %reduce-scatter.11.cloned.1.call-update) | async-done | bytes 131088 | tf_op jit(solution)/shard_map/reduce_scatter | solution.py:182
  (197 shorter events, 34.1 us)
Async XLA Ops:
  7.2 101.1 %copy-start.3 = (bf16[4,256,512]{2,1,0:T(8,128)(2,1)S(1)}, bf16[4,256,512]{2,1,0:T(8,128)(2,1)}, u32[]{:S(2)}) copy-start(bf16[4,256,512]{2,1,0:T(8,128)(2,1)} %param.21) | copy-start | bytes 3145732
  7.2 56.0 %copy-start.33 = (s32[4,256]{1,0:T(4,128)S(1)}, s32[4,256]{1,0:T(4,128)}, u32[]{:S(2)}) copy-start(s32[4,256]{1,0:T(4,128)} %param.23) | copy-start | bytes 12292
  7.2 56.0 %copy-start.37 = (s32[4]{0:T(128)S(1)}, s32[4]{0:T(128)}, u32[]{:S(2)}) copy-start(s32[4]{0:T(128)} %param.22) | copy-start | bytes 52
  7.2 56.1 %copy-start.32 = (bf16[16,512]{1,0:T(8,128)(2,1)S(1)}, bf16[16,512]{1,0:T(8,128)(2,1)}, u32[]{:S(2)}) copy-start(bf16[16,512]{1,0:T(8,128)(2,1)} %param.29) | copy-start | bytes 49156
  7.2 101.6 %all-gather.4.cloned.1.call-start = ((), (), s32[]{:S(2)}) async-start(), calls=%async_computation.4 | async-start | bytes 1622016 | tf_op jit(solution)/shard_map/all_gather | solution.py:102
  8.0 141.4 %all-gather.6.cloned.1.call-start = ((), (), s32[]{:S(2)}) async-start(), calls=%async_computation.5 | async-start | bytes 2162688 | tf_op jit(solution)/shard_map/all_gather | solution.py:136
  8.7 176.6 %all-gather.8.cloned.1.call-start = ((), (), s32[]{:S(2)}) async-start(), calls=%async_computation.6 | async-start | bytes 2162688 | tf_op jit(solution)/shard_map/all_gather | solution.py:138
  9.4 336.3 %reduce-scatter.7.cloned.1.call-start = ((), (), s32[]{:S(2)}) async-start(), calls=%async_computation.8 | async-start | bytes 1081344 | tf_op jit(solution)/shard_map/reduce_scatter | solution.py:233
  59.4 49.3 %copy-start.30 = (f32[512]{0:T(512)}, f32[512]{0:T(512)S(1)}, u32[]{:S(2)}) copy-start(f32[512]{0:T(512)S(1)} %convert_element_type.125) | copy-start | bytes 6148
  62.6 0.6 copy-start.28
  62.6 49.7 %copy-start.24 = (f32[1024]{0:T(1024)}, f32[1024]{0:T(1024)S(1)}, u32[]{:S(2)}) copy-start(f32[1024]{0:T(1024)S(1)} %rsqrt.22) | copy-start | bytes 12292
  62.6 49.7 %copy-start.26 = (f32[1,2,4,128]{3,1,2,0:T(2,128)}, f32[1,2,4,128]{3,1,2,0:T(2,128)S(1)}, u32[]{:S(2)}) copy-start(f32[1,2,4,128]{3,1,2,0:T(2,128)S(1)} %copy.97) | copy-start | bytes 12292
  108.8 3.6 copy-start.19
  124.6 2.3 copy-start.11
  133.9 1.2 copy-start.5
  138.9 1.2 copy-start.5
  147.6 1.3 copy-start
  185.3 10.4 %copy-start.1 = (f32[1024,512]{1,0:T(8,128)S(1)}, f32[1024,512]{1,0:T(8,128)}, u32[]{:S(2)}) copy-start(f32[1024,512]{1,0:T(8,128)} %copy-done) | copy-start | bytes 6291460
  185.3 10.4 %copy-start.36 = (bf16[512,2048]{1,0:T(8,128)(2,1)S(1)}, bf16[512,2048]{1,0:T(8,128)(2,1)}, u32[]{:S(2)}) copy-start(bf16[512,2048]{1,0:T(8,128)(2,1)} %all-gather.6.cloned.1.call-done) | copy-start | bytes 6291460
  195.7 2.9 copy-start.8
  198.7 1.2 copy-start.9
  199.6 1.3 copy-start.4
  199.9 1.4 copy-start.22
  200.9 2.2 copy-start.21
  211.8 238.1 %reduce-scatter.5.cloned.1.call-start = ((), (), s32[]{:S(2)}) async-start(), calls=%async_computation.7 | async-start | bytes 3244032 | tf_op jit(solution)/shard_map/reduce_scatter | solution.py:230
  213.9 1.2 copy-start.6
  213.9 1.5 copy-start.7
  218.1 1.2 copy-start.14
  218.1 2.0 copy-start.12
  220.0 1.5 copy-start.15
  220.5 1.0 copy-start.13
  223.8 1.2 copy-start.6
  223.8 1.5 copy-start.7
  227.9 1.2 copy-start.14
  228.0 2.0 copy-start.12
  229.9 1.5 copy-start.15
  230.4 1.0 copy-start.13
  233.4 5.2 copy-start.16
  243.5 2.7 copy-start.17
  246.2 1.2 copy-start.18
  246.3 2.9 copy-start.20
  247.5 1.7 copy-start.23
  252.7 1.6 copy-start.2
  252.7 340.4 %reduce-scatter.9.cloned.1.call-start = ((), (), s32[]{:S(2)}) async-start(), calls=%async_computation.9 | async-start | bytes 4325376 | tf_op jit(solution)/shard_map/reduce_scatter | solution.py:180
  261.0 472.2 %reduce-scatter.11.cloned.1.call-start = ((), (), s32[]{:S(2)}) async-start(), calls=%async_computation.10 | async-start | bytes 4325376 | tf_op jit(solution)/shard_map/reduce_scatter | solution.py:182
  267.8 0.6 copy-start.34
  267.8 4.1 copy-start.27
  267.9 4.1 copy-start.31
  271.9 4.7 copy-start.29
  271.9 6.0 copy-start.25
  276.6 1.3 copy-start.10
  323.3 4.1 copy-start.35
  323.3 5.1 copy-start.38
Sparse Core Ops, SparseCore 0:
  10.9 57.9 all-gather.3
  71.8 55.2 all-gather.5
  130.0 55.2 all-gather.7
  211.9 133.7 reduce-scatter.6
  352.5 97.4 reduce-scatter.4
  452.7 140.3 reduce-scatter.8
  596.0 137.0 reduce-scatter.10
where the time goes:
time: 747 us; the launch traced here: 740 us
  waiting for transfers between devices  430 us (58%)
  blocking collectives  126 us (17%)
  local copies, waits for them, and re-layouts  75 us (10%)
  matrix products  71.4 us (10%)
  other arithmetic  21.5 us (3%)
  between operations  15.1 us (2%)
    reduce_scatter x1, waiting for transfers between devices, shards(): lax.psum_scatter(w_up_grad, ('dp', 'shard'), scatter_dimension=0, tiled=T...  143 us
    reduce_scatter x1, waiting for transfers between devices, shards(): lax.psum_scatter(w_down_grad, ('dp', 'shard'), scatter_dimension=0, tiled...  140 us
    reduce_scatter x1, waiting for transfers between devices, shards(): lax.psum_scatter(w_qkv_grad, ('dp', 'shard'), scatter_dimension=0, tiled=...  104 us
    unnamed x2, blocking collectives  81.2 us
    all_gather x1, blocking collectives, shards(): lax.all_gather(w_out, ('dp', 'shard'), axis=0, tiled=True)  45 us
    all_gather x1, waiting for transfers between devices, shards(): lax.all_gather(w_down, ('dp', 'shard'), axis=0, tiled=True)  26.8 us
    unnamed x95, local copies, waits for them, and re-layouts  23.1 us
  transfers between devices with their start and end apart: 7, of which 5 were waited for; matrix products, arithmetic and copies ran while one was open for 17% of the time, Pallas kernels for 0%

commit v1 on v0

v1 whole, which is shorter than its diff:
```python
import functools

import jax
import jax.numpy as jnp
from jax import lax
from jax.experimental import pallas as pl
from jax.experimental.pallas import tpu as pltpu
from jax.sharding import PartitionSpec as P

HEADS = 8
HEAD_DIM = 64
SCALE = HEAD_DIM ** (-0.5)
EPS = 1e-05
MASKED = -1e30
GELU_A = 0.7978845608028654
GELU_B = GELU_A * 0.044715
MESH = pl.DeviceIdType.MESH
BF = jnp.bfloat16
F32 = jnp.float32

D = HEADS * HEAD_DIM
QUADS = 2
QW = D // QUADS
CHUNKS = 4
LN1G, LN1B, QB, VB, OB, LN2G, LN2B, DB, UPB = range(9)


def nn(a, b):
    return lax.dot_general(a, b, (((1,), (0,)), ((), ())), preferred_element_type=F32)


def nt(a, b):
    return lax.dot_general(a, b, (((1,), (1,)), ((), ())), preferred_element_type=F32)


def tn(a, b):
    return lax.dot_general(a, b, (((0,), (0,)), ((), ())), preferred_element_type=F32)


def flip(v):
    return 1 - v


class Gather:
    def __init__(self, buf, send, recv, place):
        self.buf, self.send, self.recv = buf, send, recv
        self.z, self.x, self.y, self.c = place
        self.all = []

    def _go(self, slot, src, dst_dev):
        z, x, y, c = dst_dev
        cp = pltpu.make_async_remote_copy(
            src_ref=src, dst_ref=src, send_sem=self.send.at[slot], recv_sem=self.recv.at[slot],
            device_id=(z * 2 + x, y * 2 + c), device_id_type=MESH)
        cp.start()
        self.all.append(cp)
        return cp

    def along_z(self):
        z, x, y, c = self.z, self.x, self.y, self.c
        own = self.buf.at[z, x * 2 + y, c]
        self.a = [self._go(d - 1, own, (lax.rem(z + d, 4), x, y, c)) for d in (1, 2, 3)]

    def over_xy(self):
        for cp in self.a:
            cp.wait_recv()
        z, x, y, c = self.z, self.x, self.y, self.c
        own = self.buf.at[:, x * 2 + y, c]
        self.b = [
            self._go(3, own, (z, x, flip(y), c)),
            self._go(4, own, (z, flip(x), y, c)),
            self._go(5, own, (z, flip(x), flip(y), c)),
            self._go(6, own, (z, x, y, flip(c))),
        ]

    def to_core(self):
        z, x, y, c = self.z, self.x, self.y, self.c
        self.e = []
        for i, (xx, yy) in enumerate(((x, flip(y)), (flip(x), y), (flip(x), flip(y)))):
            self.b[i].wait_recv()
            self.e.append(self._go(7 + i, self.buf.at[:, xx * 2 + yy, c], (z, x, y, flip(c))))

    def ready(self):
        self.b[3].wait_recv()
        for cp in self.e:
            cp.wait_recv()

    def finish(self):
        for cp in self.all:
            cp.wait_send()


class Scatter:
    def __init__(self, buf, bufs, send, recv, place):
        self.buf = buf
        self.rc, self.rxy, self.s2, self.rz = bufs
        self.send, self.recv = send, recv
        self.z, self.x, self.y, self.c = place
        self.all = []

    def _go(self, slot, src, dst, dst_dev):
        z, x, y, c = dst_dev
        cp = pltpu.make_async_remote_copy(
            src_ref=src, dst_ref=dst, send_sem=self.send.at[slot], recv_sem=self.recv.at[slot],
            device_id=(z * 2 + x, y * 2 + c), device_id_type=MESH)
        cp.start()
        self.all.append(cp)
        return cp

    def to_core(self, zs=None):
        z, x, y, c = self.z, self.x, self.y, self.c
        self.a = self._go(0, self.buf.at[:, :, flip(c)], self.rc, (z, x, y, flip(c)))

    def over_xy(self):
        self.a.wait_recv()
        z, x, y, c = self.z, self.x, self.y, self.c
        n = self.rc.shape[0]

        def add(i, carry):
            self.rc[i] = (self.rc[i].astype(F32) + self.buf[i, :, c].astype(F32)).astype(BF)
            return carry

        lax.fori_loop(0, n, add, 0)
        self.b = [
            self._go(1, self.rc.at[:, x * 2 + flip(y)], self.rxy.at[0], (z, x, flip(y), c)),
            self._go(2, self.rc.at[:, flip(x) * 2 + y], self.rxy.at[1], (z, flip(x), y, c)),
            self._go(3, self.rc.at[:, flip(x) * 2 + flip(y)], self.rxy.at[2], (z, flip(x), flip(y), c)),
        ]

    def along_z(self):
        for cp in self.b:
            cp.wait_recv()
        z, x, y, c = self.z, self.x, self.y, self.c
        self.sum_xy(slice(None))
        self.send_z()

    def sum_xy(self, dst):
        z, x, y, c = self.z, self.x, self.y, self.c
        r = self.rxy
        self.s2[dst] = (
            (self.rc[:, x * 2 + y].astype(F32) + r[0].astype(F32)) + (r[1].astype(F32) + r[2].astype(F32))
        ).astype(BF)

    def send_z(self):
        z, x, y, c = self.z, self.x, self.y, self.c
        self.d = []
        for k in (1, 2, 3):
            to = lax.rem(z + k, 4)
            self.d.append(self._go(3 + k, self.s2.at[to], self.rz.at[k - 1], (to, x, y, c)))

    def result(self):
        for cp in self.d:
            cp.wait_recv()
        r = self.rz
        return (self.s2[self.z].astype(F32) + r[0].astype(F32)) + (r[1].astype(F32) + r[2].astype(F32))

    def finish(self):
        for cp in self.all:
            cp.wait_send()


def layer(comm, rows, slots, ff, *refs):
    tokens = rows * slots
    fc = ff // CHUNKS
    it = iter(refs)
    take = lambda n: [next(it) for _ in range(n)]
    x_hbm, g_hbm, len_ref, ord_ref, vec_in = take(5)
    if comm:
        wqkv_s, wout_s, wup_s, wdn_s = take(4)
    else:
        w_in = take(4 + CHUNKS)
        upb_in, = take(1)
    out_hbm, ig_hbm = take(2)
    if comm:
        gqkv_o, gout_o, gup_o, gdn_o, sg_o = take(5)
    else:
        g_out = take(4 + CHUNKS)
        sg_o, = take(1)
    xv, gv, bias, h1, h1t, pt, mixed, n2, r2, h2, h2t, yacc, dh2, act_s, dpre_s, da, outv, vec, sg = take(19)
    qkv = take(QUADS)
    dproj = take(QUADS)
    w_qkv = take(QUADS)
    w_out, w_dn = take(2)
    w_up = take(CHUNKS)
    g_qkv = take(QUADS)
    g_wout, g_dn = take(2)
    g_up = take(CHUNKS)
    local, = take(1)
    dx1 = yacc

    def tok(r):
        return pl.ds(pl.multiple_of(r * slots, slots), slots)

    def rows_loop(body):
        def step(r, carry):
            body(r)
            return carry

        lax.fori_loop(0, rows, step, 0)

    copies = []

    def start(slot, src, dst):
        cp = pltpu.make_async_copy(src, dst, local.at[slot])
        cp.start()
        return cp

    cx = start(0, x_hbm, xv)
    cg = start(1, g_hbm, gv)
    if comm:
        (small, vplaced, ag_send, ag_recv, rs_send, rs_recv, sm_r, sm_send, sm_recv) = take(9)
        rs_bufs = [take(4) for _ in range(QUADS + 1 + CHUNKS)]
        rs_dn = [take(2) for _ in range(CHUNKS)]
        s2_dn, rz_dn = take(2)
        dp, sh = lax.axis_index("dp"), lax.axis_index("shard")
        z, x, y, c = lax.div(dp, 2), lax.rem(dp, 2), lax.div(sh, 2), lax.rem(sh, 2)
        place = (z, x, y, c)
        xy = x * 2 + y
        lc = []
        k = 2
        for j in range(QUADS):
            for t in range(3):
                lc.append(start(k, wqkv_s.at[:, pl.ds(t * D + j * QW, QW)], w_qkv[j].at[z, xy, c, :, pl.ds(t * QW, QW)]))
                k += 1
        lc.append(start(k, wout_s, w_out.at[z, xy, c])); k += 1
        lc.append(start(k, wdn_s, w_dn.at[z, xy, c])); k += 1
        for j in range(CHUNKS):
            lc.append(start(k, wup_s.at[:, pl.ds(j * fc, fc)], w_up[j].at[z, xy, c])); k += 1
        bar = pltpu.get_barrier_semaphore()
        for zz, xx, yy, cc in [(lax.rem(z + d, 4), x, y, c) for d in (1, 2, 3)] + [
            (z, x, flip(y), c), (z, flip(x), y, c), (z, flip(x), flip(y), c), (z, x, y, flip(c))]:
            pl.semaphore_signal(bar, 1, device_id=(zz * 2 + xx, yy * 2 + cc), device_id_type=MESH)
        row = lax.broadcasted_iota(jnp.int32, (128, 128), 0)
        lane = lax.broadcasted_iota(jnp.int32, (128, 128), 1)
        eye = (lane == row + (xy * 2 + c) * 16).astype(BF)
        eye_up = (lane == row + c * 64).astype(BF)
        v_in = vec_in[...]
        vrow = lax.broadcasted_iota(jnp.int32, (16, 128), 0)
        small[z, xy, c] = jnp.where(vrow == UPB, nn(v_in, eye_up), nn(v_in, eye)).astype(BF)
        gathers = [
            Gather(b, ag_send.at[i], ag_recv.at[i], place)
            for i, b in enumerate([small] + w_qkv + [w_out, w_dn] + w_up)
        ]
        pl.semaphore_wait(bar, 7)
        gathers[0].along_z()
        for cp in lc:
            cp.wait()
        for gth in gathers[1:]:
            gth.along_z()
        gathers[0].over_xy()
        gathers[1].over_xy()
    else:
        lc = [start(2 + i, w_in[i], b) for i, b in enumerate(w_qkv + [w_out, w_dn] + w_up)]

    kk = lax.broadcasted_iota(jnp.int32, (slots, slots), 0)
    qq = lax.broadcasted_iota(jnp.int32, (slots, slots), 1)
    for r in range(rows):
        across = jnp.broadcast_to(ord_ref[r : r + 1, :].astype(F32), (slots, slots))
        down = across.T
        ok = jnp.logical_or(jnp.logical_and(kk < len_ref[r], down <= across), kk == qq)
        bias[r] = jnp.where(ok, 0.0, MASKED)
    sg[...] = jnp.zeros_like(sg)
    cx.wait()
    if comm:
        gathers[0].to_core()
        gathers[1].to_core()
        gathers[2].over_xy()
        gathers[0].ready()
        acc = None
        for zz in range(4):
            tot = None
            for w in range(4):
                for q in range(2):
                    b = small[zz, w, q].astype(F32)
                    tot = b if tot is None else tot + b
            vec[0:16, zz * 128 : (zz + 1) * 128] = tot
            for w in range(4):
                two = (small[zz, w, 0].astype(F32) + small[zz, w, 1].astype(F32))[UPB : UPB + 1]
                vec[16 + zz : 17 + zz, w * 128 : (w + 1) * 128] = two
    else:
        vec[0:16] = vec_in[...]
        vec[16:20] = upb_in[...]

    def v(i):
        return vec[i : i + 1, :]

    def add(i, val):
        sg[i : i + 1, :] += val

    def col(val):
        return jnp.sum(val, axis=0, keepdims=True)

    def norm(val):
        centred = val - jnp.mean(val, axis=-1, keepdims=True)
        spread = jnp.mean(centred * centred, axis=-1, keepdims=True)
        r = lax.rsqrt(spread + EPS)
        return centred * r, r

    def first_norm(r):
        t = tok(r)
        n, _ = norm(xv[t].astype(F32))
        h = (n * v(LN1G) + v(LN1B)).astype(BF)
        h1[t] = h
        h1t[:, t] = h.T

    rows_loop(first_norm)
    lane = lax.broadcasted_iota(jnp.int32, (slots, 128), 1)
    first = lane < HEAD_DIM

    def heads_apart(pair):
        nil = jnp.zeros_like(pair)
        return jnp.where(first, pair, nil), jnp.where(first, nil, pair)

    for j in range(QUADS):
        if comm:
            if j + 1 < QUADS:
                gathers[1 + j + 1].to_core()
            if j == 0:
                gathers[3].over_xy()
                gathers[4].over_xy()
            else:
                gathers[5].over_xy()
            gathers[1 + j].ready()
        else:
            lc[j].wait()
        shift = jnp.concatenate(
            [v(QB)[:, j * QW : (j + 1) * QW], jnp.zeros((1, QW), F32), v(VB)[:, j * QW : (j + 1) * QW]], axis=1)
        mult = jnp.where(lax.broadcasted_iota(jnp.int32, (1, 3 * QW), 1) < QW, SCALE, 1.0)

        def attend(r, j=j, shift=shift, mult=mult):
            t = tok(r)
            w = w_qkv[j][...].reshape(D, 3 * QW)
            proj = ((nn(h1[t], w) + shift) * mult).astype(BF)
            qkv[j][t] = proj
            for p in range(QW // 128):
                s = slice(p * 128, (p + 1) * 128)
                q = proj[:, p * 128 : (p + 1) * 128]
                k = proj[:, QW + p * 128 : QW + (p + 1) * 128]
                u = proj[:, 2 * QW + p * 128 : 2 * QW + (p + 1) * 128]
                sc = nt(jnp.concatenate(heads_apart(k), axis=0), q)
                ps = []
                for h in range(2):
                    sh_ = sc[h * slots : (h + 1) * slots] + bias[r]
                    e = jnp.exp(sh_ - jnp.max(sh_, axis=0, keepdims=True))
                    ps.append((e * (1.0 / jnp.sum(e, axis=0, keepdims=True))).astype(BF))
                probs = jnp.concatenate(ps, axis=0)
                pt[j, r, p] = probs
                m = tn(probs, jnp.concatenate(heads_apart(u), axis=0))
                mixed[t, pl.ds(j * QW + p * 128, 128)] = m.astype(BF)

        rows_loop(attend)

    cg.wait()
    if comm:
        gathers[3].to_core()
        gathers[4].to_core()
        gathers[6].over_xy()
        gathers[3].ready()
    else:
        lc[QUADS].wait()

    def second_norm(r):
        t = tok(r)
        x1 = xv[t].astype(F32) + (nn(mixed[t], w_out[...].reshape(D, D)) + v(OB))
        n, rr = norm(x1)
        h = (n * v(LN2G) + v(LN2B)).astype(BF)
        h2[t] = h
        h2t[:, t] = h.T
        n2[t] = n
        r2[t] = jnp.broadcast_to(rr, (slots, 128))
        yacc[t] = x1 + v(DB)
        dh2[t] = jnp.zeros((slots, D), F32)
        add(DB, col(gv[t].astype(F32)))

    rows_loop(second_norm)
    if comm:
        gathers[4].ready()
        gathers[5].to_core()
        gathers[6].to_core()
        gathers[7].over_xy()
        gathers[8].over_xy()
        sc = []
    else:
        lc[QUADS + 1].wait()

    for j in range(CHUNKS):
        if comm:
            gathers[5 + j].ready()
            if j == 1:
                gathers[7].to_core()
                gathers[8].to_core()
        else:
            lc[QUADS + 2 + j].wait()
        ub = vec[16 + j : 17 + j, :]

        def feed(r, j=j, ub=ub):
            t = tok(r)
            wu = w_up[j][...].reshape(D, fc)
            wd = w_dn[j].reshape(fc, D)
            pre = nn(h2[t], wu) + ub
            sq = pre * pre
            th = jnp.tanh(pre * (GELU_A + GELU_B * sq))
            half = 0.5 * pre
            a = (half + half * th).astype(BF)
            slope = (0.5 + 0.5 * th) + half * (1.0 - th * th) * (GELU_A + 3.0 * GELU_B * sq)
            dpre = nt(gv[t], wd) * slope
            dl = dpre.astype(BF)
            act_s[t] = a
            dpre_s[t] = dl
            add(12 + j, col(dpre))
            yacc[t] += nn(a, wd)
            dh2[t] += nt(dl, wu)

        rows_loop(feed)
        g_dn[j] = tn(act_s[...], gv[...]).astype(BF).reshape(g_dn.shape[1:])
        g_up[j][...] = nn(h2t[...], dpre_s[...]).astype(BF).reshape(g_up[j].shape)
        if comm:
            up = Scatter(g_up[j], rs_bufs[QUADS + 1 + j], rs_send.at[j], rs_recv.at[j], place)
            dn = Scatter(g_dn.at[pl.ds(j, 1)], (rs_dn[j][0], rs_dn[j][1], s2_dn, rz_dn),
                         rs_send.at[CHUNKS + j], rs_recv.at[CHUNKS + j], place)
            up.to_core()
            dn.to_core()
            sc.append((up, dn))
            if j >= 1:
                sc[j - 1][0].over_xy()
                sc[j - 1][1].over_xy()
            if j >= 2:
                sc[j - 2][0].along_z()

    def second_back(r):
        t = tok(r)
        outv[t] = yacc[t].astype(BF)
        g2 = dh2[t]
        n = n2[t]
        add(LN2G, col(g2 * n))
        add(LN2B, col(g2))
        e = g2 * v(LN2G)
        dx = gv[t].astype(F32) + r2[t, pl.ds(0, 1)] * (
            e - jnp.mean(e, axis=-1, keepdims=True) - n * jnp.mean(e * n, axis=-1, keepdims=True))
        dx1[t] = dx
        add(OB, col(dx))
        da[t] = dx.astype(BF)

    rows_loop(second_back)
    co = start(0, outv, out_hbm)
    g_wout[...] = tn(mixed[...], da[...]).astype(BF).reshape(g_wout.shape)
    if comm:
        last = len(sc) - 1
        sc[last][0].over_xy()
        sc[last][1].over_xy()
        sc[last - 1][0].along_z()
        wo = Scatter(g_wout, rs_bufs[QUADS], rs_send.at[2 * CHUNKS], rs_recv.at[2 * CHUNKS], place)
        wo.to_core()
        sq_ = []

    for j in range(QUADS):
        def back(r, j=j):
            t = tok(r)
            wo_ = w_out[2 * j : 2 * j + 2].reshape(QW, D)
            dmix = nt(da[t], wo_).astype(BF)
            for p in range(QW // 128):
                q = qkv[j][t, pl.ds(p * 128, 128)]
                k = qkv[j][t, pl.ds(QW + p * 128, 128)]
                u = qkv[j][t, pl.ds(2 * QW + p * 128, 128)]
                dm = dmix[:, p * 128 : (p + 1) * 128]
                probs = pt[j, r, p]
                dm0, dm1 = heads_apart(dm)
                q0, q1 = heads_apart(q)
                dv = nn(probs[:slots], dm0) + nn(probs[slots:], dm1)
                dpt = nt(jnp.concatenate(heads_apart(u), axis=0), dm)
                ds = []
                for h in range(2):
                    pf = probs[h * slots : (h + 1) * slots].astype(F32)
                    d = dpt[h * slots : (h + 1) * slots]
                    ds.append((pf * (d - jnp.sum(pf * d, axis=0, keepdims=True))).astype(BF))
                dk = nn(ds[0], q0) + nn(ds[1], q1)
                dq = tn(jnp.concatenate(ds, axis=0), jnp.concatenate(heads_apart(k), axis=0)) * SCALE
                s0 = j * QW + p * 128
                sg[QB : QB + 1, s0 : s0 + 128] += col(dq)
                sg[VB : VB + 1, s0 : s0 + 128] += col(dv)
                dproj[j][t, pl.ds(p * 128, 128)] = dq.astype(BF)
                dproj[j][t, pl.ds(QW + p * 128, 128)] = dk.astype(BF)
                dproj[j][t, pl.ds(2 * QW + p * 128, 128)] = dv.astype(BF)

        rows_loop(back)
        g_qkv[j][...] = nn(h1t[...], dproj[j][...]).astype(BF).reshape(g_qkv[j].shape)
        if comm:
            one = Scatter(g_qkv[j], rs_bufs[j], rs_send.at[2 * CHUNKS + 1 + j], rs_recv.at[2 * CHUNKS + 1 + j], place)
            one.to_core()
            sq_.append(one)
            if j == 0:
                sc[last][0].along_z()
                for i, (_, dn) in enumerate(sc):
                    for cp in dn.b:
                        cp.wait_recv()
                    dn.sum_xy(pl.ds(i, 1))
                sc[last][1].send_z()
                wo.over_xy()
            else:
                sq_[0].over_xy()
                wo.along_z()
                sq_[1].over_xy()
                sq_[0].along_z()

    def first_back(r):
        t = tok(r)
        g1 = nt(dproj[0][t], w_qkv[0][...].reshape(D, 3 * QW)) + nt(dproj[1][t], w_qkv[1][...].reshape(D, 3 * QW))
        n, rr = norm(xv[t].astype(F32))
        add(LN1G, col(g1 * n))
        add(LN1B, col(g1))
        e = g1 * v(LN1G)
        dx1[t] = dx1[t] + rr * (e - jnp.mean(e, axis=-1, keepdims=True) - n * jnp.mean(e * n, axis=-1, keepdims=True))

    rows_loop(first_back)
    ci = start(1, dx1, ig_hbm)
    if comm:
        sends = []

        def swap(slot, dev):
            zz, xx, yy, cc = dev
            cp = pltpu.make_async_remote_copy(
                src_ref=sg_src.at[slot_src], dst_ref=sm_r.at[slot], send_sem=sm_send.at[slot], recv_sem=sm_recv.at[slot],
                device_id=(zz * 2 + xx, yy * 2 + cc), device_id_type=MESH)
            cp.start()
            sends.append(cp)
            return cp

        sg_src = sm_r
        slot_src = 7
        sm_r[7] = sg[...]
        one_ = swap(0, (z, x, y, flip(c)))
        one_.wait_recv()
        slot_src = 8
        sm_r[8] = sm_r[7] + sm_r[0]
        three = [swap(1, (z, x, flip(y), c)), swap(2, (z, flip(x), y, c)), swap(3, (z, flip(x), flip(y), c))]
        sq_[1].along_z()
        for cp in three:
            cp.wait_recv()
        slot_src = 9
        sm_r[9] = (sm_r[8] + sm_r[1]) + (sm_r[2] + sm_r[3])
        three = [swap(3 + k, (lax.rem(z + k, 4), x, y, c)) for k in (1, 2, 3)]
        for j in range(CHUNKS):
            gup_o[:, j * fc : (j + 1) * fc] = sc[j][0].result()
        gdn_o[...] = sc[last][1].result()
        gout_o[...] = wo.result()
        for j in range(QUADS):
            res = sq_[j].result()
            for t in range(3):
                gqkv_o[:, t * D + j * QW : t * D + (j + 1) * QW] = res[:, t * QW : (t + 1) * QW]
        for cp in three:
            cp.wait_recv()
        sg_o[...] = (sm_r[9] + sm_r[4]) + (sm_r[5] + sm_r[6])
        for gth in gathers:
            gth.finish()
        for up, dn in sc:
            up.finish()
            dn.finish()
        wo.finish()
        for one in sq_:
            one.finish()
        for cp in sends:
            cp.wait_send()
    else:
        sg_o[...] = sg[...]
        out_c = [start(2 + i, b, o) for i, (b, o) in enumerate(zip(g_qkv + [g_wout, g_dn] + g_up, g_out))]
        for cp in out_c:
            cp.wait()
    co.wait()
    ci.wait()


def run_layer(comm, rows, slots, ff, operands):
    tokens = rows * slots
    fc = ff // CHUNKS
    blk = lambda r, c: (4, 4, 2, r, c)
    pieces = [blk(D // 32, 3 * QW)] * QUADS + [blk(D // 32, D), blk(ff // 32, D)] + [blk(D // 32, fc)] * CHUNKS
    any_ = pl.BlockSpec(memory_space=pl.ANY)
    vm = pl.BlockSpec(memory_space=pltpu.VMEM)
    smem = pl.BlockSpec(memory_space=pltpu.SMEM)
    in_specs = [any_, any_, smem, vm, vm]
    out_shape = [jax.ShapeDtypeStruct((tokens, D), BF), jax.ShapeDtypeStruct((tokens, D), F32)]
    out_specs = [any_, any_]
    if comm:
        in_specs += [any_] * 4
        out_shape += [jax.ShapeDtypeStruct(s, F32) for s in ((D // 32, 3 * D), (D // 32, D), (D // 32, ff), (ff // 32, D))]
        out_specs += [vm] * 4
    else:
        in_specs += [any_] * len(pieces) + [vm]
        out_shape += [jax.ShapeDtypeStruct(s, BF) for s in pieces]
        out_specs += [any_] * len(pieces)
    out_shape.append(jax.ShapeDtypeStruct((16, D), F32))
    out_specs.append(vm)
    V = pltpu.VMEM
    scratch = [
        V((tokens, D), BF), V((tokens, D), BF), V((rows, slots, slots), F32), V((tokens, D), BF), V((D, tokens), BF),
        V((QUADS, rows, QW // 128, 2 * slots, slots), BF), V((tokens, D), BF), V((tokens, D), F32), V((tokens, 128), F32),
        V((tokens, D), BF), V((D, tokens), BF), V((tokens, D), F32), V((tokens, D), F32), V((tokens, fc), BF),
        V((tokens, fc), BF), V((tokens, D), BF), V((tokens, D), BF), V((24, D), F32), V((16, D), F32),
    ]
    scratch += [V((tokens, 3 * QW), BF)] * (2 * QUADS)
    scratch += [V(s, BF) for s in pieces] * 2
    scratch += [pltpu.SemaphoreType.DMA((24,))]
    if comm:
        n_ag, n_rs = len(pieces) + 1, 2 * CHUNKS + 1 + QUADS
        dma = pltpu.SemaphoreType.DMA
        scratch += [V(blk(16, 128), BF), V((16, 128), BF), dma((n_ag, 10)), dma((n_ag, 10)), dma((n_rs, 7)), dma((n_rs, 7)),
                    V((10, 16, D), F32), dma((7,)), dma((7,))]
        for s in pieces[:QUADS] + [pieces[QUADS]] + pieces[QUADS + 2 :]:
            r, c = s[3:]
            scratch += [V((4, 4, r, c), BF), V((3, 4, r, c), BF), V((4, r, c), BF), V((3, r, c), BF)]
        r, c = pieces[QUADS + 1][3:]
        for _ in range(CHUNKS):
            scratch += [V((1, 4, r, c), BF), V((3, 1, r, c), BF)]
        scratch += [V((4, r, c), BF), V((3, r, c), BF)]
    return pl.pallas_call(
        functools.partial(layer, comm, rows, slots, ff),
        out_shape=out_shape, in_specs=in_specs, out_specs=out_specs, scratch_shapes=scratch,
        compiler_params=pltpu.CompilerParams(
            vmem_limit_bytes=63 << 20, **(dict(collective_id=0, has_side_effects=True) if comm else {})),
        cost_estimate=pl.CostEstimate(flops=22_000_000_000, bytes_accessed=6 << 20, transcendentals=4 << 20),
    )(*operands)


def shards(
    inputs, lengths, slot_order, ln1_gain, ln1_bias, w_qkv, q_bias, v_bias, w_out, out_bias, ln2_gain, ln2_bias, w_up, up_bias,
    w_down, down_bias, cotangent, fast=True,
):
    rows, slots, width = inputs.shape
    tokens = rows * slots
    flat = (inputs.reshape(tokens, width), cotangent.reshape(tokens, width), lengths, slot_order)
    vectors = [ln1_gain, ln1_bias, q_bias, v_bias, out_bias, ln2_gain, ln2_bias, down_bias, up_bias]
    axes = ("dp", "shard")
    me = lax.axis_index(axes)
    n = lax.axis_size(axes)
    if fast:
        ff = w_up.shape[1]
        packed = jnp.stack([jnp.pad(a, (0, 128 - a.shape[0])) for a in vectors] + [jnp.zeros((128,), BF)] * 7)
        out, ig, gqkv, gout, gup, gdn, sg = run_layer(
            True, rows, slots, ff, flat + (packed, w_qkv, w_out, w_up, w_down))
        mine = lax.dynamic_slice(sg, (0, me * (width // n)), (8, width // n))
        upb = lax.dynamic_slice(sg[12:16].reshape(-1), (me * (ff // n),), (ff // n,))
    else:
        ff = w_up.shape[1]
        full = lambda a: lax.all_gather(a, axes, axis=0, tiled=True)
        whole = [full(a).astype(F32) for a in vectors]
        packed = jnp.stack(whole[:8] + [jnp.zeros((width,), F32)] * 8)
        wq, wo, wu, wd = full(w_qkv), full(w_out), full(w_up), full(w_down)
        fc = ff // CHUNKS
        cut = lambda a: a.reshape(4, 4, 2, a.shape[0] // 32, a.shape[1])
        pieces = [cut(jnp.concatenate([wq[:, t * D + j * QW : t * D + (j + 1) * QW] for t in range(3)], axis=1)) for j in range(QUADS)]
        pieces += [cut(wo), cut(wd)] + [cut(wu[:, j * fc : (j + 1) * fc]) for j in range(CHUNKS)]
        res = run_layer(False, rows, slots, ff, flat + (packed, *pieces, whole[8].reshape(CHUNKS, fc)))
        out, ig, sg = res[0], res[1], res[-1]
        back = [r.astype(F32).reshape(-1, r.shape[-1]) for r in res[2:-1]]
        own = lambda a: lax.psum_scatter(a, axes, scatter_dimension=0, tiled=True)
        gq = jnp.stack(back[:QUADS]).reshape(QUADS, D, 3, QW).transpose(1, 2, 0, 3).reshape(D, 3 * D)
        gqkv, gout, gdn, gup = own(gq), own(back[QUADS]), own(back[QUADS + 1]), own(jnp.concatenate(back[QUADS + 2 :], axis=1))
        mine = own(sg[0:8].T).T
        upb = own(sg[12:16].reshape(-1))
    shape = (rows, slots, width)
    return (
        out.reshape(shape), ig.reshape(shape), mine[LN1G], mine[LN1B], gqkv, mine[QB], mine[VB], gout, mine[OB], mine[LN2G],
        mine[LN2B], gup, upb, gdn, mine[DB],
    )


def solution(mesh):
    whole = P(("dp", "shard"))
    fast = mesh.shape["dp"] == 8 and mesh.shape["shard"] == 4
    return jax.shard_map(
        functools.partial(shards, fast=fast), mesh=mesh, in_specs=(whole,) * 17, out_specs=(whole,) * 15, check_vma=False)
```

time: 747 us -> 125 us (0.17)
  waiting for transfers between devices: 430 us -> 0 us
  blocking collectives: 126 us -> 0 us
  Pallas kernels: 0 us -> 110 us
  matrix products: 71.4 us -> 0 us
  local copies, waits for them, and re-layouts: 75 us -> 13.5 us
  other arithmetic: 21.5 us -> 0 us
  between operations: 15.1 us -> 0.7 us
    reduce_scatter x4 -> x0, waiting for transfers between devices: 401 us -> none  [the longest x1 143 us: shards(): lax.psum_scatter(w_up_grad, ('dp', 'shard'), scatter_dimension=0, tiled=T...]
    pallas_call x0 -> x1, Pallas kernels: none -> 110 us  [run_layer(): pl.pallas_call(functools.partial(layer, comm, rows, slots, ff), out_shape...]
    unnamed x2 -> x0, blocking collectives: 81.2 us -> none
    dot_general x26 -> x0, matrix products: 71.4 us -> none  [the longest x1 10.4 us: shards(): jnp.einsum('to,fo->tf', grad_down, mlp_back[4], preferred_element_type=jn...]
    all_gather x1 -> x0, blocking collectives: 45 us -> none  [shards(): lax.all_gather(w_out, ('dp', 'shard'), axis=0, tiled=True)]
    all_gather x3 -> x0, waiting for transfers between devices: 26.8 us -> none  [the longest x1 26.8 us: shards(): lax.all_gather(w_down, ('dp', 'shard'), axis=0, tiled=True)]
    reshape x10 -> x0, local copies, waits for them, and re-layouts: 21.8 us -> none  [the longest x1 3.91 us: shards(): grad_mixed.reshape(block_shape)]
    while x34 -> x0, local copies, waits for them, and re-layouts: 21.4 us -> none  [the longest x3 9.84 us: shards(): lax.map(attend_back, (query_blocks, key_blocks, value_blocks, grad_mixed....]
  transfers between devices with their start and end apart: 7 -> 0, of which waited for: 5 -> 0; matrix products, arithmetic and copies ran while one was open for 17% -> 0% of each run, Pallas kernels for 0% -> 0%
where the time goes in v1:
time: 125 us
  Pallas kernels  110 us (88%)
  local copies, waits for them, and re-layouts  13.5 us (11%)
    pallas_call x1, Pallas kernels, run_layer(): pl.pallas_call(functools.partial(layer, comm, rows, slots, ff), out_shape...  110 us
    unnamed x18, local copies, waits for them, and re-layouts  6.89 us
    another operation x9, local copies, waits for them, and re-layouts, shards(): jnp.stack([jnp.pad(a, (0, 128 - a.shape[0])) for a in vectors] + [jnp.zer...  4.58 us

profile of v1, /device:TPU:0, one launch (start us, length us, event | category | flops | bytes accessed | tf_op | source)
XLA Modules:
  0.0 124.6 jit_solution(16237417767809029635)
XLA Ops:
  0.6 0.7 pad_bitcast_fusion
  1.3 0.7 pad_bitcast_fusion.2
  2.0 0.7 pad_bitcast_fusion.4
  2.7 0.7 pad_bitcast_fusion.6
  3.4 0.7 pad_bitcast_fusion.8
  4.0 1.2 stack.47.refs_4_
  5.2 110.4 %shard_map.280 = (bf16[1024,512]{1,0:T(8,128)(2,1)}, f32[1024,512]{1,0:T(8,128)}, f32[16,1536]{1,0:T(8,128)}, f32[16,512]{1,0:T(8,128)}, f32[16,2048]{1,0:T(8,12...) custom-call(bf16[1024,512]{1,0:T(8,128)(2,1)} %bitcast.44, bf16[1024,512]{1,0:T(8,128)(2,1)} %bitcast.45, s32[4]{0:T(128)} %refs_2_.1, ...), custom_call_target="tpu_custom_call" | custom-call | flops 22000001024 | bytes 6291456 | tf_op jit(solution)/shard_map/pallas_call | solution.py:615
  115.6 0.0 copy-start
  115.6 0.9 constant_dynamic-slice_fusion
  116.5 0.5 slice_bitcast_fusion.1
  117.1 0.7 slice_bitcast_fusion
  117.8 0.6 dynamic_slice.7
  118.4 2.3 %copy.39 = bf16[4,256,512]{2,1,0:T(8,128)(2,1)} copy(bf16[4,256,512]{2,1,0:T(8,128)(2,1)} %bitcast.42) | data formatting | bytes 2097152
  120.7 0.0 copy-done
  120.7 0.0 copy-start.3
  120.7 0.0 copy-start.4
  120.7 0.0 copy-start.2
  120.7 0.0 copy-start.1
  120.7 1.3 %copy.40 = f32[4,256,512]{2,1,0:T(8,128)} copy(f32[4,256,512]{2,1,0:T(8,128)S(1)} %bitcast.41) | data formatting | bytes 4194304
  122.0 0.0 copy-done.3
  122.0 0.6 copy.41
  122.6 0.0 copy-done.4
  122.7 0.6 copy.42
  123.3 0.0 copy-done.2
  123.3 0.7 copy.43
  123.9 0.0 copy-done.1
  123.9 0.7 copy.44
  (4 shorter events, 0.0 us)
Async XLA Ops:
  115.6 5.0 %copy-start = (f32[1024,512]{1,0:T(8,128)S(1)}, f32[1024,512]{1,0:T(8,128)}, u32[]{:S(2)}) copy-start(f32[1024,512]{1,0:T(8,128)} %get-tuple-element.23) | copy-start | bytes 6291460
  120.7 1.3 %copy-start.3 = (f32[16,1536]{1,0:T(8,128)S(1)}, f32[16,1536]{1,0:T(8,128)}, u32[]{:S(2)}) copy-start(f32[16,1536]{1,0:T(8,128)} %get-tuple-element.64) | copy-start | bytes 294916
  120.7 2.0 %copy-start.4 = (f32[16,512]{1,0:T(8,128)S(1)}, f32[16,512]{1,0:T(8,128)}, u32[]{:S(2)}) copy-start(f32[16,512]{1,0:T(8,128)} %get-tuple-element.67) | copy-start | bytes 98308
  120.7 2.6 %copy-start.2 = (f32[16,2048]{1,0:T(8,128)S(1)}, f32[16,2048]{1,0:T(8,128)}, u32[]{:S(2)}) copy-start(f32[16,2048]{1,0:T(8,128)} %get-tuple-element.71) | copy-start | bytes 393220
  120.7 3.3 %copy-start.1 = (f32[64,512]{1,0:T(8,128)S(1)}, f32[64,512]{1,0:T(8,128)}, u32[]{:S(2)}) copy-start(f32[64,512]{1,0:T(8,128)} %get-tuple-element.73) | copy-start | bytes 393220

commit v2 on v1

v2 whole, which is shorter than its diff:
```python
import functools
import types

import jax
import jax.numpy as jnp
from jax import lax
from jax.experimental import pallas as pl
from jax.experimental.pallas import tpu as pltpu
from jax.sharding import PartitionSpec as P

HEADS = 8
HEAD_DIM = 64
SCALE = HEAD_DIM ** (-0.5)
EPS = 1e-05
MASKED = -1e30
GELU_A = 0.7978845608028654
GELU_B = GELU_A * 0.044715
MESH = pl.DeviceIdType.MESH
BF = jnp.bfloat16
F32 = jnp.float32

D = HEADS * HEAD_DIM
GROUPS = ((0, 256), (256, 256))
CHUNKS = 4
LN1G, LN1B, QB, VB, OB, LN2G, LN2B, DB, UPB = range(9)
LATE = (LN1G, LN1B, QB, VB)
EARLY = (OB, LN2G, LN2B, DB)


def nn(a, b):
    return lax.dot_general(a, b, (((1,), (0,)), ((), ())), preferred_element_type=F32)


def nt(a, b):
    return lax.dot_general(a, b, (((1,), (1,)), ((), ())), preferred_element_type=F32)


def tn(a, b):
    return lax.dot_general(a, b, (((0,), (0,)), ((), ())), preferred_element_type=F32)


def nothing():
    pass


class Node:
    def __getattr__(self, name):
        return nothing


def plan(x):
    return types.SimpleNamespace(
        start=(x.sm.zgo, x.g[0].zgo, x.g[1].zgo, x.out.zgo, x.u[0].zgo, x.dn.zgo, x.u[1].zgo, x.u[2].zgo, x.u[3].zgo,),
        pre=(x.sm.xy, x.g[0].xy, x.sm.turn, x.sm.core, x.sm.ready,),
        proj=(x.g[1].xy, x.out.xy, x.g[0].turn, x.u[0].xy, x.g[0].core, x.g[0].ready, x.g[1].turn, x.d[0].xy, x.out.turn, x.u[1].xy, x.d[1].xy, x.g[1].core, x.g[1].ready,),
        attend={0: (x.u[0].turn, x.u[2].xy,), 1: (x.out.core, x.d[0].turn, x.u[1].turn, x.d[2].xy, x.u[3].xy,)},
        second_norm={0: (x.out.ready, x.u[0].core, x.d[1].turn, x.u[2].turn, x.d[3].xy, x.d[0].core,), 1: (x.u[1].core,)},
        feed=(
            {0: (x.u[0].ready, x.d[0].ready,), 1: (x.d[2].turn,)},
            {0: (x.u[1].ready, x.d[1].ready,), 1: (x.d[2].core, x.d[3].turn,)},
            {0: (x.u[2].ready, x.d[2].ready,), 1: (x.d[3].core, x.sd[0].xy,)},
            {0: (x.u[3].ready, x.d[3].ready,), 1: (x.sd[0].turn, x.sd[1].xy,)},
        ),
        fed=((x.d[1].core, x.u[3].turn, x.u[2].core,), (x.u[3].core, x.sd[0].core, x.su[0].core,), (x.su[0].xy, x.sd[1].core, x.su[1].core,), (x.su[0].turn, x.su[1].xy, x.sd[2].core, x.su[2].core,)),
        gdn=(),
        gup=(x.sd[0].sum, x.sd[3].core,),
        second_back={0: (x.sd[1].turn, x.sd[2].xy, x.su[3].core,), 1: (x.su[2].xy,)},
        gwout=(x.te.go, x.su[0].sum, x.su[1].turn, x.sd[3].xy, x.su[3].xy,),
        back=({0: (x.su[3].turn, x.sq[1].core, x.te.end,), 1: (x.sd[2].sum, x.su[2].sum, x.so.turn, x.sq[1].xy,)}, {0: (x.so.core,), 1: (x.sd[1].sum, x.sd[2].turn, x.su[2].turn, x.so.xy, x.te.turn,)}),
        gqkv=((x.sd[3].sum, x.su[3].sum, x.su[1].end,), (x.su[1].sum, x.sd[3].turn, x.su[0].end,)),
        first_back={0: (x.so.sum, x.sq[0].core,), 1: (x.sq[0].xy, x.su[2].end,)},
        tail=(x.tl.go, x.sq[1].sum, x.tl.turn, x.sq[0].sum, x.su[3].end, x.dw.end, x.so.end, x.sq[1].end, x.tl.end, x.sq[0].end,),
    )


def direct_of(x):
    return (x.sm, x.g[0], x.sq[0], x.sq[1],)


def scatter_direct(n_groups):
    return (0, 1,)


class Place:
    def __init__(self):
        dp, sh = lax.axis_index("dp"), lax.axis_index("shard")
        self.z, x, y, self.c = lax.div(dp, 2), lax.rem(dp, 2), lax.div(sh, 2), lax.rem(sh, 2)
        nx, ny, self.nc = 1 - x, 1 - y, 1 - self.c
        self.own, self.ix, self.iy, self.id = x * 2 + y, nx * 2 + y, x * 2 + ny, nx * 2 + ny
        self.zs = [lax.rem(self.z + k, 4) for k in (1, 2, 3)]
        at = lambda z, x, y, c: (z * 2 + x, y * 2 + c)
        self.dev_z = [at(k, x, y, self.c) for k in self.zs]
        self.dev_x, self.dev_y = at(self.z, nx, y, self.c), at(self.z, x, ny, self.c)
        self.dev_d, self.dev_c = at(self.z, nx, ny, self.c), at(self.z, x, y, self.nc)
        self.others = [self.dev_x, self.dev_y, self.dev_d, self.dev_c, at(self.z, nx, y, self.nc), at(self.z, x, ny, self.nc),
                       at(self.z, nx, ny, self.nc)]
        self.bytes = {}

    def send(self, src, dst, out, land, device):
        at = lambda pair: pair[0].at[pair[1]]
        cp = pltpu.make_async_remote_copy(
            src_ref=at(src), dst_ref=at(dst), send_sem=at(out), recv_sem=at(land), device_id=device, device_id_type=MESH)
        cp.start()
        n = 1
        for k in cp.src_ref.shape:
            n *= k
        key = (id(out[0]), *out[1])
        self.bytes[key] = self.bytes.get(key, 0) + n * jnp.dtype(cp.src_ref.dtype).itemsize


ALL = slice(None)
TWO, THREE, FOUR = pl.ds(0, 2), pl.ds(0, 3), pl.ds(0, 4)


def wait_for(like, sem):
    ref = like[0].at[like[1]]
    pltpu.make_async_copy(ref, ref, sem[0].at[sem[1]]).wait()


class GatherZ:
    def __init__(self, me, buf, out, land):
        self.me, self.buf, self.out, self.land = me, buf, out, land

    def go(self):
        me = self.me
        own = (self.buf, (me.z, me.own, me.c))
        for k in range(3):
            me.send(own, own, self.out, self.land, me.dev_z[k])

    def wait(self):
        wait_for((self.buf, (THREE, 0, 0)), self.land)


class Gather:
    def __init__(self, me, buf, outs, land, direct=False, zs=ALL):
        self.me, self.buf, self.direct, self.zs = me, buf, direct, zs
        self.out, self.out_core = outs
        self.land = [(land[0], (*land[1], k)) for k in range(3)]

    def line(self, i, cols=None):
        return self.buf, (self.zs, i, self.me.c) + (() if cols is None else (ALL, cols))

    def to(self, line, k, device):
        self.me.send(line, line, self.out_core if k == 2 else self.out, self.land[k], device)

    def xy(self):
        me, own = self.me, self.line(self.me.own)
        self.to(own, 0, me.dev_x)
        self.to(own, 0, me.dev_y)
        if self.direct:
            self.to(own, 1, me.dev_d)
        self.to(own, 2, me.dev_c)

    def turn(self):
        me = self.me
        wait_for((self.buf, (self.zs, TWO, 0)), self.land[0])
        if not self.direct:
            h = self.buf.shape[-1] // 2
            self.to(self.line(me.ix, pl.ds(0, h)), 1, me.dev_y)
            self.to(self.line(me.iy, pl.ds(h, h)), 1, me.dev_x)
        self.to(self.line(me.ix), 2, me.dev_c)
        self.to(self.line(me.iy), 2, me.dev_c)

    def core(self):
        wait_for((self.buf, (self.zs, 0, 0)), self.land[1])
        self.to(self.line(self.me.id), 2, self.me.dev_c)

    def ready(self):
        wait_for((self.buf, (self.zs, FOUR, 0)), self.land[2])


class Scatter:
    def __init__(self, me, buf, bufs, outs, land, direct=False, zs=ALL):
        self.me, self.buf, self.direct, self.zs = me, buf, direct, zs
        self.out_core, self.out = outs
        self.rc, self.r1, self.r2, self.s2 = bufs
        self.land = [(land[0], (*land[1], k)) for k in range(3)]
        self.h = buf.shape[-1] // 2

    def core(self):
        me = self.me
        me.send((self.buf, (self.zs, ALL, me.nc)), (self.rc, (ALL,)), self.out_core, self.land[0], me.dev_c)

    def to(self, where, cols, dst, k, device):
        me = self.me
        me.send((self.rc, (ALL, where) + (() if cols is None else (ALL, cols))), dst, self.out, self.land[k], device)

    def xy(self):
        me, h, rc, r1, r2 = self.me, self.h, self.rc, self.r1, self.r2
        wait_for((rc, (ALL,)), self.land[0])
        first = 0 if self.zs == ALL else self.zs.start
        for i in range(rc.shape[0]):
            rc[i] = rc[i] + self.buf[first + i, :, me.c]
        if self.direct:
            self.to(me.ix, None, (r2, (0,)), 2, me.dev_x)
            self.to(me.iy, None, (r2, (1,)), 2, me.dev_y)
            self.to(me.id, None, (r1, (ALL,)), 2, me.dev_d)
        else:
            lo, hi = pl.ds(0, h), pl.ds(h, h)
            self.to(me.id, lo, (r1, (0,)), 1, me.dev_x)
            self.to(me.id, hi, (r1, (1,)), 1, me.dev_y)
            self.to(me.ix, lo, (r2, (0, ALL, ALL, lo)), 2, me.dev_x)
            self.to(me.iy, hi, (r2, (1, ALL, ALL, hi)), 2, me.dev_y)

    def turn(self):
        me, h, rc, r1, r2 = self.me, self.h, self.rc, self.r1, self.r2
        wait_for((r1, (ALL,)), self.land[1])
        rc[:, me.iy, :, :h] = rc[:, me.iy, :, :h] + r1[0]
        rc[:, me.ix, :, h:] = rc[:, me.ix, :, h:] + r1[1]
        lo, hi = pl.ds(0, h), pl.ds(h, h)
        self.to(me.iy, lo, (r2, (1, ALL, ALL, lo)), 2, me.dev_y)
        self.to(me.ix, hi, (r2, (0, ALL, ALL, hi)), 2, me.dev_x)

    def sum(self):
        f = lambda v: v.astype(F32)
        if self.direct:
            wait_for((self.rc, (ALL, THREE)), self.land[2])
        else:
            wait_for((self.r2, (ALL,)), self.land[2])
        tot = f(self.rc[:, self.me.own]) + (f(self.r2[0]) + f(self.r2[1]))
        if self.direct:
            tot = tot + f(self.r1[...])
        self.s2[self.zs] = tot.astype(BF)


class ScatterZ:
    def __init__(self, me, s2, rz, out, land):
        self.me, self.s2, self.rz, self.out, self.land = me, s2, rz, out, land

    def go(self):
        me = self.me
        for k in range(3):
            me.send((self.s2, (me.zs[k],)), (self.rz, (k,)), self.out, self.land, me.dev_z[k])

    def result(self):
        wait_for((self.rz, (ALL,)), self.land)
        f = lambda v: v.astype(F32)
        return (f(self.s2[self.me.z]) + f(self.rz[0])) + (f(self.rz[1]) + f(self.rz[2]))


class Total:
    def __init__(self, me, buf, sems):
        self.me, self.buf = me, buf
        self.sem = [(sems, (k,)) for k in range(4)]

    def go(self):
        for i, d in enumerate(self.me.others):
            self.me.send((self.buf, (0,)), (self.buf, (2 + i,)), self.sem[0], self.sem[1], d)

    def turn(self):
        me, b = self.me, self.buf
        wait_for((b, (pl.ds(2, 7),)), self.sem[1])
        b[1] = ((b[0] + b[2]) + (b[3] + b[4])) + ((b[5] + b[6]) + (b[7] + b[8]))
        for k in range(3):
            me.send((b, (1,)), (b, (9 + k,)), self.sem[2], self.sem[3], me.dev_z[k])

    def result(self):
        b = self.buf
        wait_for((b, (pl.ds(9, 3),)), self.sem[3])
        return (b[1] + b[9]) + (b[10] + b[11])

    def finish(self):
        wait_for((self.buf, (pl.ds(2, 7),)), self.sem[0])
        wait_for((self.buf, (pl.ds(9, 3),)), self.sem[2])


def layer(comm, rows, slots, ff, *refs):
    tokens = rows * slots
    fc = ff // CHUNKS
    it = iter(refs)
    take = lambda n: [next(it) for _ in range(n)]
    n_groups = len(GROUPS)
    n_pieces = n_groups + 2 + CHUNKS
    x_hbm, g_hbm, len_ref, ord_ref = take(4)
    if comm:
        vec_in = take(9)
        wqkv_s, wout_s, wup_s, wdn_s = take(4)
    else:
        vec_in, = take(1)
        w_in = take(n_pieces)
        upb_in, = take(1)
    out_hbm, ig_hbm = take(2)
    if comm:
        gqkv_o, gout_o, gup_o, gdn_o, sg_o, upb_o = take(6)
    else:
        g_out = take(n_pieces)
        sg_o, = take(1)
    xv, gv, bias, h1, h1t, pt, mixed, n2, r2, h2, h2t, x1v, dx1, dh2, act, dpre_s, da, outv, vec, sg = take(20)
    qkv = take(n_groups)
    dproj = take(n_groups)
    w_qkv = take(n_groups)
    w_out, w_dn = take(2)
    w_up = take(CHUNKS)
    g_qkv = take(n_groups)
    g_wout, g_dn = take(2)
    g_up = take(CHUNKS)
    local, = take(1)
    x = types.SimpleNamespace(
        sm=Node(), g=[Node() for _ in GROUPS], out=Node(), dn=Node(), u=[Node() for _ in range(CHUNKS)], d=[Node() for _ in range(CHUNKS)],
        sq=[Node() for _ in GROUPS], so=Node(), su=[Node() for _ in range(CHUNKS)], sd=[Node() for _ in range(CHUNKS)], dw=Node(),
        te=Node(), tl=Node())

    def tok(r):
        return pl.ds(pl.multiple_of(r * slots, slots), slots)

    def now(todo):
        for f in todo:
            f()

    def rows_loop(body, ticks={}, unroll=1, also=None):
        def step(i, carry):
            if comm:
                for k in ticks:

                    @pl.when(i == k)
                    def _(k=k):
                        now(ticks[k])

            for u in range(unroll):
                body(i * unroll + u)
            if also is not None:
                also(i)
            return carry

        lax.fori_loop(0, rows // unroll, step, 0)

    def start(slot, src, dst):
        cp = pltpu.make_async_copy(src, dst, local.at[slot])
        cp.start()
        return cp

    cx = start(0, x_hbm, xv)
    cg = start(1, g_hbm, gv)
    if comm:
        small, early, late, sem_out, sem_z, sem_x, sem_s, sem_sz, sem_e, sem_l = take(10)
        rs_bufs = [take(4) for _ in range(n_groups + 1 + CHUNKS)]
        dn_bufs = [take(3) for _ in range(CHUNKS)]
        s2_dn, = take(1)
        rzs = take(n_groups + 2 + CHUNKS)
        me = Place()
        mine = (me.z, me.own, me.c)
        bar = pltpu.get_barrier_semaphore()
        for dev in me.others + me.dev_z:
            pl.semaphore_signal(bar, 1, device_id=dev, device_id_type=MESH)
        k = 2
        lc = []
        for j, (off, w) in enumerate(GROUPS):
            for t in range(3):
                start(k, wqkv_s.at[:, pl.ds(t * D + off, w)], w_qkv[j].at[(*mine, slice(None), pl.ds(t * w, w))])
            lc.append((w_qkv[j], k))
            k += 1
        for src, dst in [(wout_s, w_out), (wdn_s, w_dn)] + [(wup_s.at[:, pl.ds(j * fc, fc)], w_up[j]) for j in range(CHUNKS)]:
            start(k, src, dst.at[mine])
            lc.append((dst, k))
            k += 1
        late[12] = jnp.zeros((16, 128), F32)
        for i, r in enumerate(vec_in):
            late[12, i : i + 1, 0 : r.shape[0]] = r[...].astype(F32).reshape(1, r.shape[0])
        up_row = lax.broadcasted_iota(jnp.int32, (16, 128), 0) == UPB
        given = late[12]
        small[mine] = jnp.where(
            up_row, pltpu.roll(given, me.c * 64, 1), pltpu.roll(given, (me.own * 2 + me.c) * 16, 1)).astype(BF)

        arrived = []
        n_x = 0
        nodes = x.g + [x.out, x.dn] + x.u + [x.sm]
        for i, (node, buf) in enumerate(zip(nodes, [*w_qkv, w_out, w_dn, *w_up, small])):
            is_small = node is x.sm
            gz = GatherZ(me, buf, (sem_out, (4 if is_small else 0,)), (sem_z, (i,)))

            def zgo(i=i, gz=gz):
                if i < len(lc):
                    wait_for((lc[i][0], mine), (local, (lc[i][1],)))
                gz.go()

            node.zgo = zgo
            for j, part in enumerate(x.d if node is x.dn else [node]):
                gt = Gather(me, buf, [(sem_out, (k,)) for k in ((5, 6) if is_small else (0, 1))], (sem_x, (n_x,)), part in direct_of(x),
                            pl.ds(j, 1) if node is x.dn else ALL)
                n_x += 1

                def first(gt=gt, gz=gz):
                    if gz not in arrived:
                        arrived.append(gz)
                        gz.wait()
                    gt.xy()

                part.xy, part.turn, part.core, part.ready = first, gt.turn, gt.core, gt.ready

        def scatter(node, i, buf, four, zs=ALL):
            sc = Scatter(me, buf, four, ((sem_out, (2,)), (sem_out, (3,))), (sem_s, (i,)), node in direct_of(x), zs)
            node.core, node.xy, node.turn = sc.core, sc.xy, sc.turn
            return sc

        for i, (node, b) in enumerate(zip(x.sq + [x.so] + x.su, [*g_qkv, g_wout, *g_up])):
            sc = scatter(node, i, b, rs_bufs[i])
            node.last = ScatterZ(me, sc.s2, rzs[i], (sem_out, (3,)), (sem_sz, (i,)))

            def total(sc=sc, node=node):
                sc.sum()
                node.last.go()

            node.sum = total
        x.dw.last = ScatterZ(me, s2_dn, rzs[-1], (sem_out, (3,)), (sem_sz, (n_groups + 1 + CHUNKS,)))
        summed = []
        for j, node in enumerate(x.sd):
            sc = scatter(node, n_groups + 1 + CHUNKS + j, g_dn, (*dn_bufs[j], s2_dn), pl.ds(j, 1))

            def total(sc=sc):
                sc.sum()
                summed.append(0)
                if len(summed) == CHUNKS:
                    x.dw.last.go()

            node.sum = total

        def r_qkv(j):
            off, w = GROUPS[j]
            res = x.sq[j].last.result()
            for t in range(3):
                gqkv_o[:, t * D + off : t * D + off + w] = res[:, t * w : (t + 1) * w]

        def r_up(j):
            gup_o[:, j * fc : (j + 1) * fc] = x.su[j].last.result()

        def r_dn():
            gdn_o[...] = x.dw.last.result()

        def r_out():
            gout_o[...] = x.so.last.result()

        te, tl = Total(me, early, sem_e), Total(me, late, sem_l)

        def te_go():
            for i, r in enumerate(EARLY):
                for q in range(4):
                    early[0, 4 * i + q : 4 * i + q + 1, :] = sg[r : r + 1, q * 128 : (q + 1) * 128]
            for q in range(4):
                for w in range(4):
                    early[0, 16 + 4 * q + w : 17 + 4 * q + w, :] = sg[12 + q : 13 + q, w * 128 : (w + 1) * 128]
            te.go()

        def tl_go():
            for i, r in enumerate(LATE):
                for q in range(4):
                    late[0, 4 * i + q : 4 * i + q + 1, :] = sg[r : r + 1, q * 128 : (q + 1) * 128]
            tl.go()

        shift = lax.rem(128 - (me.own * 2 + me.c) * 16, 128)

        def r_early():
            e = te.result()
            early[12] = pltpu.roll(e, shift, 1)
            early[13] = pltpu.roll(e, lax.rem(128 - me.c * 64, 128), 1)
            for i, r in enumerate(EARLY):
                sg_o[r : r + 1, :] = early[12, pl.ds(4 * i + me.z, 1), :]
            upb_o[...] = early[13, pl.ds(16 + 4 * me.z + me.own, 1), :]

        def r_late():
            late[12] = pltpu.roll(tl.result(), shift, 1)
            for i, r in enumerate(LATE):
                sg_o[r : r + 1, :] = late[12, pl.ds(4 * i + me.z, 1), :]

        x.te.go, x.te.turn, x.te.end = te_go, te.turn, r_early
        x.tl.go, x.tl.turn, x.tl.end = tl_go, tl.turn, r_late
        x.dw.end, x.so.end = r_dn, r_out
        for j in range(n_groups):
            x.sq[j].end = functools.partial(r_qkv, j)
        for j in range(CHUNKS):
            x.su[j].end = functools.partial(r_up, j)
        pl.semaphore_wait(bar, 10)
    else:
        lc = [start(2 + i, w_in[i], b) for i, b in enumerate(w_qkv + [w_out, w_dn] + w_up)]
    t_ = plan(x)
    now(t_.start)

    kk = lax.broadcasted_iota(jnp.int32, (slots, slots), 0)
    qq = lax.broadcasted_iota(jnp.int32, (slots, slots), 1)

    def masks(r):
        across = jnp.broadcast_to(ord_ref[pl.ds(r, 1), :].astype(F32), (slots, slots))
        down = across.T
        ok = jnp.logical_or(jnp.logical_and(kk < len_ref[r], down <= across), kk == qq)
        bias[r] = jnp.where(ok, 0.0, MASKED)

    rows_loop(masks)
    sg[...] = jnp.zeros_like(sg)
    cx.wait()

    def v(i):
        return vec[i : i + 1, :]

    def add(i, val):
        sg[i : i + 1, :] += val

    def col(val):
        return jnp.sum(val, axis=0, keepdims=True)

    def norm(val):
        centred = val - jnp.mean(val, axis=-1, keepdims=True)
        spread = jnp.mean(centred * centred, axis=-1, keepdims=True)
        r = lax.rsqrt(spread + EPS)
        return centred * r, r

    now(t_.pre)
    if comm:
        for zz in range(4):
            tot = None
            for w in range(4):
                for q in range(2):
                    b = small[zz, w, q].astype(F32)
                    tot = b if tot is None else tot + b
            vec[0:16, zz * 128 : (zz + 1) * 128] = tot
            for w in range(4):
                two = (small[zz, w, 0].astype(F32) + small[zz, w, 1].astype(F32))[UPB : UPB + 1]
                vec[16 + zz : 17 + zz, w * 128 : (w + 1) * 128] = two
    else:
        vec[0:16] = vec_in[...]
        vec[16:20] = upb_in[...]

    def first_norm(r):
        t = tok(r)
        n, _ = norm(xv[t].astype(F32))
        h = (n * v(LN1G) + v(LN1B)).astype(BF)
        h1[t] = h
        h1t[:, t] = h.T

    rows_loop(first_norm, unroll=2)
    lane = lax.broadcasted_iota(jnp.int32, (slots, 128), 1)
    first_half = lane < HEAD_DIM

    def heads_apart(pair):
        nil = jnp.zeros_like(pair)
        return jnp.where(first_half, pair, nil), jnp.where(first_half, nil, pair)

    now(t_.proj)
    shifts, mults = [], []
    for j, (off, w) in enumerate(GROUPS):
        if not comm:
            lc[j].wait()
        shifts.append(
            jnp.concatenate([v(QB)[:, off : off + w], jnp.zeros((1, w), F32), v(VB)[:, off : off + w]], axis=1))
        mults.append(jnp.where(lax.broadcasted_iota(jnp.int32, (1, 3 * w), 1) < w, SCALE, 1.0))

    def attend(r):
        t = tok(r)
        for j, (off, w) in enumerate(GROUPS):
            proj = ((nn(h1[t], w_qkv[j][...].reshape(D, 3 * w)) + shifts[j]) * mults[j]).astype(BF)
            qkv[j][t] = proj
            for p in range(w // 128):
                q = proj[:, p * 128 : (p + 1) * 128]
                k = proj[:, w + p * 128 : w + (p + 1) * 128]
                u = proj[:, 2 * w + p * 128 : 2 * w + (p + 1) * 128]
                sc = nt(jnp.concatenate(heads_apart(k), axis=0), q)
                ps = []
                for h in range(2):
                    sh = sc[h * slots : (h + 1) * slots] + bias[r]
                    e = jnp.exp(sh - jnp.max(sh, axis=0, keepdims=True))
                    ps.append((e * (1.0 / jnp.sum(e, axis=0, keepdims=True))).astype(BF))
                probs = jnp.concatenate(ps, axis=0)
                pt[r, off // 128 + p] = probs
                m = tn(probs, jnp.concatenate(heads_apart(u), axis=0))
                mixed[t, pl.ds(off + p * 128, 128)] = m.astype(BF)

    rows_loop(attend, t_.attend, unroll=2)
    cg.wait()
    if not comm:
        lc[n_groups].wait()

    def second_norm(r):
        t = tok(r)
        x1 = xv[t].astype(F32) + (nn(mixed[t], w_out[...].reshape(D, D)) + v(OB))
        n, rr = norm(x1)
        h = (n * v(LN2G) + v(LN2B)).astype(BF)
        h2[t] = h
        h2t[:, t] = h.T
        n2[t] = n
        r2[t] = jnp.broadcast_to(rr, (slots, 128))
        x1v[t] = x1
        add(DB, col(gv[t].astype(F32)))

    rows_loop(second_norm, t_.second_norm, unroll=2)
    if not comm:
        lc[n_groups + 1].wait()

    for j in range(CHUNKS):
        if not comm:
            lc[n_groups + 2 + j].wait()
        ub = vec[16 + j : 17 + j, :]

        def feed(r, j=j, ub=ub):
            t = tok(r)
            wu = w_up[j][...].reshape(D, fc)
            wd = w_dn[j].reshape(fc, D)
            pre = nn(h2[t], wu) + ub
            sq_ = pre * pre
            c1 = 0.5 + 0.5 * jnp.tanh(pre * (GELU_A + GELU_B * sq_))
            a = pre * c1
            slope = c1 + a * ((1.0 - c1) * (2.0 * GELU_A + 6.0 * GELU_B * sq_))
            dpre = nt(gv[t], wd) * slope
            dl = dpre.astype(BF)
            act[pl.ds(pl.multiple_of(j * tokens + r * slots, slots), slots)] = a.astype(BF)
            dpre_s[pl.ds(pl.multiple_of((j % 2) * tokens + r * slots, slots), slots)] = dl
            add(12 + j, col(dpre))
            back = nt(dl, wu)
            dh2[t] = back if j == 0 else dh2[t] + back

        def grads(i, j=j - 1):
            cut = pl.ds(pl.multiple_of(i * (fc // 2), fc // 2), fc // 2)
            g = tn(act[j * tokens : (j + 1) * tokens, cut], gv[...])
            g_dn[j, pl.ds(2 * i, 2)] = g.astype(BF).reshape(2, *g_dn.shape[2:])
            cut = pl.ds(pl.multiple_of(i * (D // 2), D // 2), D // 2)
            g = nn(h2t[cut], dpre_s[(j % 2) * tokens : (j % 2 + 1) * tokens])
            g_up[j][pl.ds(2 * i, 2)] = g.astype(BF).reshape(2, *g_up[j].shape[1:])

        rows_loop(feed, t_.feed[j], unroll=2, also=grads if j else None)
        now(t_.fed[j])
    j = CHUNKS - 1
    now(t_.gdn)
    g_dn[j] = tn(act[j * tokens : (j + 1) * tokens], gv[...]).astype(BF).reshape(g_dn.shape[1:])
    now(t_.gup)
    g_up[j][...] = nn(h2t[...], dpre_s[(j % 2) * tokens : (j % 2 + 1) * tokens]).astype(BF).reshape(g_up[j].shape)

    def second_back(r):
        t = tok(r)
        g2 = dh2[t]
        n = n2[t]
        add(LN2G, col(g2 * n))
        add(LN2B, col(g2))
        e = g2 * v(LN2G)
        dx = gv[t].astype(F32) + r2[t, pl.ds(0, 1)] * (
            e - jnp.mean(e, axis=-1, keepdims=True) - n * jnp.mean(e * n, axis=-1, keepdims=True))
        dx1[t] = dx
        add(OB, col(dx))
        da[t] = dx.astype(BF)

    rows_loop(second_back, t_.second_back, unroll=2)
    now(t_.gwout)
    g_wout[...] = tn(mixed[...], da[...]).astype(BF).reshape(g_wout.shape)

    for j in reversed(range(n_groups)):
        off, w = GROUPS[j]

        def back(r, j=j, off=off, w=w):
            t = tok(r)
            wo_ = w_out[...].reshape(D, D)[off : off + w]
            dmix = nt(da[t], wo_).astype(BF)
            for p in range(w // 128):
                q = qkv[j][t, pl.ds(p * 128, 128)]
                k = qkv[j][t, pl.ds(w + p * 128, 128)]
                u = qkv[j][t, pl.ds(2 * w + p * 128, 128)]
                dm = dmix[:, p * 128 : (p + 1) * 128]
                probs = pt[r, off // 128 + p]
                dm0, dm1 = heads_apart(dm)
                q0, q1 = heads_apart(q)
                dv = nn(probs[:slots], dm0) + nn(probs[slots:], dm1)
                dpt = nt(jnp.concatenate(heads_apart(u), axis=0), dm)
                ds = []
                for h in range(2):
                    pf = probs[h * slots : (h + 1) * slots].astype(F32)
                    d = dpt[h * slots : (h + 1) * slots]
                    ds.append((pf * (d - jnp.sum(pf * d, axis=0, keepdims=True))).astype(BF))
                dk = nn(ds[0], q0) + nn(ds[1], q1)
                dq = tn(jnp.concatenate(ds, axis=0), jnp.concatenate(heads_apart(k), axis=0)) * SCALE
                s0 = off + p * 128
                sg[QB : QB + 1, s0 : s0 + 128] += col(dq)
                sg[VB : VB + 1, s0 : s0 + 128] += col(dv)
                dproj[j][t, pl.ds(p * 128, 128)] = dq.astype(BF)
                dproj[j][t, pl.ds(w + p * 128, 128)] = dk.astype(BF)
                dproj[j][t, pl.ds(2 * w + p * 128, 128)] = dv.astype(BF)

        rows_loop(back, t_.back[j], unroll=2)
        now(t_.gqkv[j])
        g_qkv[j][...] = nn(h1t[...], dproj[j][...]).astype(BF).reshape(g_qkv[j].shape)

    def first_back(r):
        t = tok(r)
        g1 = None
        for j, (off, w) in enumerate(GROUPS):
            part = nt(dproj[j][t], w_qkv[j][...].reshape(D, 3 * w))
            g1 = part if g1 is None else g1 + part
        n, rr = norm(xv[t].astype(F32))
        add(LN1G, col(g1 * n))
        add(LN1B, col(g1))
        e = g1 * v(LN1G)
        dx1[t] = dx1[t] + rr * (e - jnp.mean(e, axis=-1, keepdims=True) - n * jnp.mean(e * n, axis=-1, keepdims=True))
        y = x1v[t] + v(DB)
        for j in range(CHUNKS):
            y = y + nn(act[pl.ds(pl.multiple_of(j * tokens + r * slots, slots), slots)], w_dn[j].reshape(fc, D))
        outv[t] = y.astype(BF)

    rows_loop(first_back, t_.first_back, unroll=2)
    ci = start(1, dx1, ig_hbm)
    co = start(0, outv, out_hbm)
    now(t_.tail)
    if comm:
        for k in range(4):
            room = me.bytes[id(sem_out), k] // (D * 2)
            wait_for((act, (pl.ds(0, room),)), (sem_out, (k,)))
        wait_for((small, (THREE, 0, 0)), (sem_out, (4,)))
        wait_for((small, (ALL, THREE, 0)), (sem_out, (5,)))
        wait_for((small, (ALL, FOUR, 0)), (sem_out, (6,)))
        te.finish()
        tl.finish()
    else:
        sg_o[...] = sg[...]
        out_c = [start(2 + i, b, o) for i, (b, o) in enumerate(zip(g_qkv + [g_wout, g_dn] + g_up, g_out))]
        for cp in out_c:
            cp.wait()
    co.wait()
    ci.wait()


def run_layer(comm, rows, slots, ff, operands):
    tokens = rows * slots
    fc = ff // CHUNKS
    n_groups = len(GROUPS)
    blk = lambda r, c: (4, 4, 2, r, c)
    pieces = [blk(D // 32, 3 * w) for _, w in GROUPS] + [blk(D // 32, D), blk(ff // 32, D)] + [blk(D // 32, fc)] * CHUNKS
    any_ = pl.BlockSpec(memory_space=pl.ANY)
    vm = pl.BlockSpec(memory_space=pltpu.VMEM)
    smem = pl.BlockSpec(memory_space=pltpu.SMEM)
    in_specs = [any_, any_, smem, vm] + [vm] * (9 if comm else 1)
    out_shape = [jax.ShapeDtypeStruct((tokens, D), BF), jax.ShapeDtypeStruct((tokens, D), F32)]
    out_specs = [any_, any_]
    if comm:
        in_specs += [any_] * 4
        out_shape += [jax.ShapeDtypeStruct(s, F32) for s in (
            (D // 32, 3 * D), (D // 32, D), (D // 32, ff), (ff // 32, D), (8, 128), (1, 128))]
        out_specs += [vm] * 6
    else:
        in_specs += [any_] * len(pieces) + [vm]
        out_shape += [jax.ShapeDtypeStruct(s, BF) for s in pieces] + [jax.ShapeDtypeStruct((16, D), F32)]
        out_specs += [any_] * len(pieces) + [vm]
    V = pltpu.VMEM
    scratch = [
        V((tokens, D), BF), V((tokens, D), BF), V((rows, slots, slots), F32), V((tokens, D), BF), V((D, tokens), BF),
        V((rows, D // 128, 2 * slots, slots), BF), V((tokens, D), BF), V((tokens, D), F32), V((tokens, 128), F32),
        V((tokens, D), BF), V((D, tokens), BF), V((tokens, D), F32), V((tokens, D), F32), V((tokens, D), F32),
        V((CHUNKS * tokens, fc), BF), V((2 * tokens, fc), BF), V((tokens, D), BF), V((tokens, D), BF), V((24, D), F32), V((16, D), F32),
    ]
    scratch += [V((tokens, 3 * w), BF) for _, w in GROUPS] * 2
    scratch += [V(s, BF) for s in pieces] * 2
    scratch += [pltpu.SemaphoreType.DMA((2 + len(pieces),))]
    if comm:
        dma = pltpu.SemaphoreType.DMA
        n_xy = n_groups + 1 + 2 * CHUNKS
        n_z = len(pieces) + 1
        scratch += [V(blk(16, 128), BF), V((14, 32, 128), F32), V((13, 16, 128), F32)]
        scratch += [dma((7,)), dma((n_z,)), dma((n_xy + 1, 3)), dma((n_xy, 3)), dma((n_z,)), dma((4,)), dma((4,))]
        whole = pieces[: n_groups + 1] + pieces[n_groups + 2 :]
        by_way = lambda straight, z, r, c: V((z, r, c) if straight else (2, z, r, c // 2), BF)
        straight = scatter_direct(n_groups)
        for i, s in enumerate(whole):
            r, c = s[3:]
            scratch += [V((4, 4, r, c), BF), by_way(i in straight, 4, r, c), V((2, 4, r, c), BF), V((4, r, c), BF)]
        r, c = pieces[n_groups + 1][3:]
        for j in range(CHUNKS):
            scratch += [V((1, 4, r, c), BF), by_way(len(whole) + j in straight, 1, r, c), V((2, 1, r, c), BF)]
        scratch += [V((4, r, c), BF)]
        scratch += [V((3, *s[3:]), BF) for s in whole] + [V((3, r, c), BF)]
    return pl.pallas_call(
        functools.partial(layer, comm, rows, slots, ff),
        out_shape=out_shape, in_specs=in_specs, out_specs=out_specs, scratch_shapes=scratch,
        compiler_params=pltpu.CompilerParams(
            vmem_limit_bytes=63 << 20, **(dict(collective_id=0, has_side_effects=True) if comm else {})),
        cost_estimate=pl.CostEstimate(flops=22_000_000_000, bytes_accessed=6 << 20, transcendentals=4 << 20),
    )(*operands)


def deliver(n, *refs):
    ins, outs, bufs, sems = refs[: n + 2], refs[n + 2 : n + 2 + n + 9], refs[n + 2 + n + 9 : -1], refs[-1]
    parts = []
    for i in range(n):
        rows = ins[i].shape[0]
        step = min(rows, 256)
        parts += [(i, pl.ds(k, step)) for k in range(0, rows, step)]
    first = [pltpu.make_async_copy(ins[i].at[s], bufs[i].at[s], sems.at[0, k]) for k, (i, s) in enumerate(parts)]
    second = [pltpu.make_async_copy(bufs[i].at[s], outs[i].at[s], sems.at[1, k]) for k, (i, s) in enumerate(parts)]
    for cp in first:
        cp.start()
    for i in range(9):
        o = outs[n + i]
        k = o.shape[0]
        o[...] = (ins[n][i : i + 1, 0:k] if i < 8 else ins[n + 1][:, 0:k]).reshape(k)
    for a, b in zip(first, second):
        a.wait()
        b.start()
    for cp in second:
        cp.wait()


def run_deliver(share, up_share, results):
    n = len(results) - 2
    any_ = pl.BlockSpec(memory_space=pl.ANY)
    vm = pl.BlockSpec(memory_space=pltpu.VMEM)
    n_parts = sum(max(1, r.shape[0] // 256) for r in results[:n])
    return pl.pallas_call(
        functools.partial(deliver, n),
        out_shape=[jax.ShapeDtypeStruct(r.shape, r.dtype) for r in results[:n]]
        + [jax.ShapeDtypeStruct((share,), F32)] * 8 + [jax.ShapeDtypeStruct((up_share,), F32)],
        in_specs=[any_] * n + [vm, vm], out_specs=[any_] * n + [vm] * 9,
        scratch_shapes=[pltpu.VMEM(r.shape, r.dtype) for r in results[:n]] + [pltpu.SemaphoreType.DMA((2, n_parts))],
        compiler_params=pltpu.CompilerParams(vmem_limit_bytes=63 << 20),
    )(*results)


def shards(
    inputs, lengths, slot_order, ln1_gain, ln1_bias, w_qkv, q_bias, v_bias, w_out, out_bias, ln2_gain, ln2_bias, w_up, up_bias,
    w_down, down_bias, cotangent, fast=True,
):
    rows, slots, width = inputs.shape
    tokens = rows * slots
    ff = w_up.shape[1]
    flat = (inputs.reshape(tokens, width), cotangent.reshape(tokens, width), lengths, slot_order)
    vectors = [ln1_gain, ln1_bias, q_bias, v_bias, out_bias, ln2_gain, ln2_bias, down_bias, up_bias]
    axes = ("dp", "shard")
    if fast:
        res = run_layer(True, rows, slots, ff, flat + (*vectors, w_qkv, w_out, w_up, w_down))
        out, ig, gqkv, gout, gup, gdn, *mine, upb = run_deliver(ln1_gain.shape[0], up_bias.shape[0], res)
    else:
        full = lambda a: lax.all_gather(a, axes, axis=0, tiled=True)
        whole = [full(a).astype(F32) for a in vectors]
        packed = jnp.stack(whole[:8] + [jnp.zeros((width,), F32)] * 8)
        wq, wo, wu, wd = full(w_qkv), full(w_out), full(w_up), full(w_down)
        fc = ff // CHUNKS
        cut = lambda a: a.reshape(4, 4, 2, a.shape[0] // 32, a.shape[1])
        pieces = [cut(jnp.concatenate([wq[:, t * D + off : t * D + off + w] for t in range(3)], axis=1)) for off, w in GROUPS]
        pieces += [cut(wo), cut(wd)] + [cut(wu[:, j * fc : (j + 1) * fc]) for j in range(CHUNKS)]
        res = run_layer(False, rows, slots, ff, flat + (packed, *pieces, whole[8].reshape(CHUNKS, fc)))
        out, ig, sg = res[0], res[1], res[-1]
        back = [r.astype(F32).reshape(-1, r.shape[-1]) for r in res[2:-1]]
        own = lambda a: lax.psum_scatter(a, axes, scatter_dimension=0, tiled=True)
        k = len(GROUPS)
        gq = jnp.concatenate([back[j][:, t * w : (t + 1) * w] for t in range(3) for j, (_, w) in enumerate(GROUPS)], axis=1)
        gqkv, gout, gdn, gup = own(gq), own(back[k]), own(back[k + 1]), own(jnp.concatenate(back[k + 2 :], axis=1))
        mine = own(sg[0:8].T).T
        upb = own(sg[12:16].reshape(-1))
    shape = (rows, slots, width)
    return (
        out.reshape(shape), ig.reshape(shape), mine[LN1G], mine[LN1B], gqkv, mine[QB], mine[VB], gout, mine[OB], mine[LN2G],
        mine[LN2B], gup, upb, gdn, mine[DB],
    )


def solution(mesh):
    whole = P(("dp", "shard"))
    fast = mesh.shape["dp"] == 8 and mesh.shape["shard"] == 4
    return jax.shard_map(
        functools.partial(shards, fast=fast), mesh=mesh, in_specs=(whole,) * 17, out_specs=(whole,) * 15, check_vma=False)
```

time: 125 us -> 93.3 us (0.75)
  Pallas kernels: 110 us -> 92.3 us
  local copies, waits for them, and re-layouts: 13.5 us -> 0 us
    pallas_call x1, Pallas kernels: 110 us -> 88 us  [run_layer(): pl.pallas_call(functools.partial(layer, comm, rows, slots, ff), out_shape...]
    unnamed x18 -> x0, local copies, waits for them, and re-layouts: 6.89 us -> none
    another operation x9 -> x0, local copies, waits for them, and re-layouts: 4.58 us -> none  [shards(): jnp.stack([jnp.pad(a, (0, 128 - a.shape[0])) for a in vectors] + [jnp.zer...]
    pallas_call x0 -> x1, Pallas kernels: none -> 4.26 us  [run_deliver(): pl.pallas_call(functools.partial(deliver, n), out_shape=[jax.ShapeDtypeSt...]
    dynamic_slice x2 -> x0, local copies, waits for them, and re-layouts: 1.48 us -> none  [the longest x1 0.9 us: shards(): mine = lax.dynamic_slice(sg, (0, me * (width // n)), (8, width // n))]
where the time goes in v2:
time: 93.3 us; the launch traced here: 93.1 us
  Pallas kernels  92.3 us (99%)
    pallas_call x1, Pallas kernels, run_layer(): pl.pallas_call(functools.partial(layer, comm, rows, slots, ff), out_shape...  88 us
    pallas_call x1, Pallas kernels, run_deliver(): pl.pallas_call(functools.partial(deliver, n), out_shape=[jax.ShapeDtypeSt...  4.26 us

profile of v2, /device:TPU:0, one launch (start us, length us, event | category | flops | bytes accessed | tf_op | source)
XLA Modules:
  0.0 93.1 jit_solution(14586180091811675676)
XLA Ops:
  0.7 88.0 %shard_map.280 = (bf16[1024,512]{1,0:T(8,128)(2,1)}, f32[1024,512]{1,0:T(8,128)}, f32[16,1536]{1,0:T(8,128)}, f32[16,512]{1,0:T(8,128)}, f32[16,2048]{1,0:T(8,12...) custom-call(bf16[1024,512]{1,0:T(8,128)(2,1)} %bitcast.5, bf16[1024,512]{1,0:T(8,128)(2,1)} %bitcast.6, ...), custom_call_target="tpu_custom_call" | custom-call | flops 22000001024 | bytes 6291456 | tf_op jit(solution)/shard_map/pallas_call | solution.py:762
  88.7 4.3 %shard_map.281 = (bf16[1024,512]{1,0:T(8,128)(2,1)}, f32[1024,512]{1,0:T(8,128)}, f32[16,1536]{1,0:T(8,128)}, f32[16,512]{1,0:T(8,128)}, f32[16,2048]{1,0:T(8,12...) custom-call(bf16[1024,512]{1,0:T(8,128)(2,1)} %get-tuple-element.38., ...), custom_call_target="tpu_custom_call" | custom-call | tf_op jit(solution)/shard_map/pallas_call | solution.py:798

commit v3 on v2

--- a/solution.py
+++ b/solution.py
@@ -52,16 +52,16 @@
     return types.SimpleNamespace(
         start=(x.sm.zgo, x.g[0].zgo, x.g[1].zgo, x.out.zgo, x.u[0].zgo, x.dn.zgo, x.u[1].zgo, x.u[2].zgo, x.u[3].zgo,),
         pre=(x.sm.xy, x.g[0].xy, x.sm.turn, x.sm.core, x.sm.ready,),
-        proj=(x.g[1].xy, x.out.xy, x.g[0].turn, x.u[0].xy, x.g[0].core, x.g[0].ready, x.g[1].turn, x.d[0].xy, x.out.turn, x.u[1].xy, x.d[1].xy, x.g[1].core, x.g[1].ready,),
-        attend={0: (x.u[0].turn, x.u[2].xy,), 1: (x.out.core, x.d[0].turn, x.u[1].turn, x.d[2].xy, x.u[3].xy,)},
-        second_norm={0: (x.out.ready, x.u[0].core, x.d[1].turn, x.u[2].turn, x.d[3].xy, x.d[0].core,), 1: (x.u[1].core,)},
+        proj=((x.g[1].xy, x.out.xy, x.g[0].turn, x.u[0].xy, x.g[0].core, x.g[0].ready,), (x.u[0].turn, x.d[1].xy, x.g[1].core, x.g[1].ready,)),
+        attend=({1: (x.g[1].turn, x.d[0].xy, x.out.turn, x.u[1].xy,)}, {1: (x.out.core, x.d[0].turn, x.u[2].xy,)}),
+        second_norm={0: (x.out.ready, x.u[0].core, x.u[1].turn, x.d[1].turn, x.d[2].xy, x.u[3].xy,), 1: (x.d[0].core,)},
         feed=(
-            {0: (x.u[0].ready, x.d[0].ready,), 1: (x.d[2].turn,)},
-            {0: (x.u[1].ready, x.d[1].ready,), 1: (x.d[2].core, x.d[3].turn,)},
-            {0: (x.u[2].ready, x.d[2].ready,), 1: (x.d[3].core, x.sd[0].xy,)},
+            {0: (x.u[0].ready, x.d[0].ready, x.u[2].turn, x.d[3].xy,), 1: (x.u[1].core, x.d[1].core,)},
+            {0: (x.u[1].ready, x.d[1].ready,), 1: (x.u[2].core, x.u[3].turn,)},
+            {0: (x.u[2].ready, x.d[2].ready,), 1: (x.u[3].core, x.sd[0].xy, x.su[0].xy, x.d[3].core,)},
             {0: (x.u[3].ready, x.d[3].ready,), 1: (x.sd[0].turn, x.sd[1].xy,)},
         ),
-        fed=((x.d[1].core, x.u[3].turn, x.u[2].core,), (x.u[3].core, x.sd[0].core, x.su[0].core,), (x.su[0].xy, x.sd[1].core, x.su[1].core,), (x.su[0].turn, x.su[1].xy, x.sd[2].core, x.su[2].core,)),
+        fed=((x.d[2].turn,), (x.d[2].core, x.d[3].turn, x.sd[0].core, x.su[0].core,), (x.sd[1].core, x.su[1].core,), (x.su[0].turn, x.su[1].xy, x.sd[2].core, x.su[2].core,)),
         gdn=(),
         gup=(x.sd[0].sum, x.sd[3].core,),
         second_back={0: (x.sd[1].turn, x.sd[2].xy, x.su[3].core,), 1: (x.su[2].xy,)},
@@ -533,19 +533,16 @@
         nil = jnp.zeros_like(pair)
         return jnp.where(first_half, pair, nil), jnp.where(first_half, nil, pair)
 
-    now(t_.proj)
-    shifts, mults = [], []
     for j, (off, w) in enumerate(GROUPS):
+        now(t_.proj[j])
         if not comm:
             lc[j].wait()
-        shifts.append(
-            jnp.concatenate([v(QB)[:, off : off + w], jnp.zeros((1, w), F32), v(VB)[:, off : off + w]], axis=1))
-        mults.append(jnp.where(lax.broadcasted_iota(jnp.int32, (1, 3 * w), 1) < w, SCALE, 1.0))
-
-    def attend(r):
-        t = tok(r)
-        for j, (off, w) in enumerate(GROUPS):
-            proj = ((nn(h1[t], w_qkv[j][...].reshape(D, 3 * w)) + shifts[j]) * mults[j]).astype(BF)
+        shift_ = jnp.concatenate([v(QB)[:, off : off + w], jnp.zeros((1, w), F32), v(VB)[:, off : off + w]], axis=1)
+        mult = jnp.where(lax.broadcasted_iota(jnp.int32, (1, 3 * w), 1) < w, SCALE, 1.0)
+
+        def attend(r, j=j, off=off, w=w, shift_=shift_, mult=mult):
+            t = tok(r)
+            proj = ((nn(h1[t], w_qkv[j][...].reshape(D, 3 * w)) + shift_) * mult).astype(BF)
             qkv[j][t] = proj
             for p in range(w // 128):
                 q = proj[:, p * 128 : (p + 1) * 128]
@@ -562,7 +559,7 @@
                 m = tn(probs, jnp.concatenate(heads_apart(u), axis=0))
                 mixed[t, pl.ds(off + p * 128, 128)] = m.astype(BF)
 
-    rows_loop(attend, t_.attend, unroll=2)
+        rows_loop(attend, t_.attend[j], unroll=2)
     cg.wait()
     if not comm:
         lc[n_groups].wait()

time: 93.3 us -> 91.8 us (0.984)
  Pallas kernels: 92.3 us -> 90.7 us
    pallas_call x1, Pallas kernels: 88 us -> 86.5 us  [run_layer(): pl.pallas_call(functools.partial(layer, comm, rows, slots, ff), out_shape...]
where the time goes in v3:
time: 91.8 us; the launch traced here: 91.5 us
  Pallas kernels  90.7 us (99%)
    pallas_call x1, Pallas kernels, run_layer(): pl.pallas_call(functools.partial(layer, comm, rows, slots, ff), out_shape...  86.5 us
    pallas_call x1, Pallas kernels, run_deliver(): pl.pallas_call(functools.partial(deliver, n), out_shape=[jax.ShapeDtypeSt...  4.26 us

profile of v3, /device:TPU:0, one launch (start us, length us, event | category | flops | bytes accessed | tf_op | source)
XLA Modules:
  0.0 91.5 jit_solution(14052330229010387002)
XLA Ops:
  0.7 86.5 %shard_map.280 = (bf16[1024,512]{1,0:T(8,128)(2,1)}, f32[1024,512]{1,0:T(8,128)}, f32[16,1536]{1,0:T(8,128)}, f32[16,512]{1,0:T(8,128)}, f32[16,2048]{1,0:T(8,12...) custom-call(bf16[1024,512]{1,0:T(8,128)(2,1)} %bitcast.5, bf16[1024,512]{1,0:T(8,128)(2,1)} %bitcast.6, ...), custom_call_target="tpu_custom_call" | custom-call | flops 22000001024 | bytes 6291456 | tf_op jit(solution)/shard_map/pallas_call | solution.py:759
  87.1 4.3 %shard_map.281 = (bf16[1024,512]{1,0:T(8,128)(2,1)}, f32[1024,512]{1,0:T(8,128)}, f32[16,1536]{1,0:T(8,128)}, f32[16,512]{1,0:T(8,128)}, f32[16,2048]{1,0:T(8,12...) custom-call(bf16[1024,512]{1,0:T(8,128)(2,1)} %get-tuple-element.38., ...), custom_call_target="tpu_custom_call" | custom-call | tf_op jit(solution)/shard_map/pallas_call | solution.py:795

commit v4 on v3

--- a/solution.py
+++ b/solution.py
@@ -62,14 +62,12 @@
             {0: (x.u[3].ready, x.d[3].ready,), 1: (x.sd[0].turn, x.sd[1].xy,)},
         ),
         fed=((x.d[2].turn,), (x.d[2].core, x.d[3].turn, x.sd[0].core, x.su[0].core,), (x.sd[1].core, x.su[1].core,), (x.su[0].turn, x.su[1].xy, x.sd[2].core, x.su[2].core,)),
-        gdn=(),
-        gup=(x.sd[0].sum, x.sd[3].core,),
-        second_back={0: (x.sd[1].turn, x.sd[2].xy, x.su[3].core,), 1: (x.su[2].xy,)},
-        gwout=(x.te.go, x.su[0].sum, x.su[1].turn, x.sd[3].xy, x.su[3].xy,),
-        back=({0: (x.su[3].turn, x.sq[1].core, x.te.end,), 1: (x.sd[2].sum, x.su[2].sum, x.so.turn, x.sq[1].xy,)}, {0: (x.so.core,), 1: (x.sd[1].sum, x.sd[2].turn, x.su[2].turn, x.so.xy, x.te.turn,)}),
-        gqkv=((x.sd[3].sum, x.su[3].sum, x.su[1].end,), (x.su[1].sum, x.sd[3].turn, x.su[0].end,)),
-        first_back={0: (x.so.sum, x.sq[0].core,), 1: (x.sq[0].xy, x.su[2].end,)},
-        tail=(x.tl.go, x.sq[1].sum, x.tl.turn, x.sq[0].sum, x.su[3].end, x.dw.end, x.so.end, x.sq[1].end, x.tl.end, x.sq[0].end,),
+        second_back={1: (x.sd[0].sum,)},
+        after=(x.te.go, x.sd[1].turn, x.sd[2].xy, x.su[2].xy, x.su[0].sum, x.sd[3].core, x.su[3].core,),
+        back=({0: (x.su[1].sum, x.sd[3].turn, x.sq[1].core, x.te.end,), 1: (x.sd[2].sum, x.su[3].turn, x.so.xy, x.sq[1].xy,)}, {1: (x.sd[1].sum, x.su[1].turn, x.sd[3].xy, x.su[3].xy, x.te.turn,)}),
+        gqkv=((x.su[2].sum, x.sd[3].sum,), (x.sd[2].turn, x.su[2].turn, x.so.core, x.su[0].end,)),
+        first_back={0: (x.su[3].sum, x.so.turn, x.sq[0].core, x.su[1].end,), 1: (x.sq[0].xy,)},
+        tail=(x.tl.go, x.sq[1].sum, x.so.sum, x.tl.turn, x.sq[0].sum, x.su[2].end, x.su[3].end, x.dw.end, x.so.end, x.sq[1].end, x.tl.end, x.sq[0].end,),
     )
 
 
@@ -271,9 +269,9 @@
     take = lambda n: [next(it) for _ in range(n)]
     n_groups = len(GROUPS)
     n_pieces = n_groups + 2 + CHUNKS
-    x_hbm, g_hbm, len_ref, ord_ref = take(4)
+    x_hbm, g_hbm, len_hbm, ord_hbm = take(4)
     if comm:
-        vec_in = take(9)
+        vec_hbm = take(9)
         wqkv_s, wout_s, wup_s, wdn_s = take(4)
     else:
         vec_in, = take(1)
@@ -281,11 +279,11 @@
         upb_in, = take(1)
     out_hbm, ig_hbm = take(2)
     if comm:
-        gqkv_o, gout_o, gup_o, gdn_o, sg_o, upb_o = take(6)
+        results = take(6)
     else:
         g_out = take(n_pieces)
         sg_o, = take(1)
-    xv, gv, bias, h1, h1t, pt, mixed, n2, r2, h2, h2t, x1v, dx1, dh2, act, dpre_s, da, outv, vec, sg = take(20)
+    xv, gv, bias, h1, h1t, pt, mixed, n2, r2, h2, h2t, x1v, dx1, dh2, act, dpre_s, da, outv, vec, sg, len_ref, ord_ref = take(22)
     qkv = take(n_groups)
     dproj = take(n_groups)
     w_qkv = take(n_groups)
@@ -331,7 +329,17 @@
 
     cx = start(0, x_hbm, xv)
     cg = start(1, g_hbm, gv)
+    n_l = 2 + n_pieces
+    cl = [start(n_l, len_hbm, len_ref), start(n_l + 1, ord_hbm, ord_ref)]
     if comm:
+        gqkv_o, gout_o, gup_o, gdn_o, sg_o, upb_o = held = take(6)
+        vec_in = take(9)
+        cv = [start(n_l + 2 + i, a, b) for i, (a, b) in enumerate(zip(vec_hbm, vec_in))]
+        given_back = []
+
+        def hand(i):
+            given_back.append(start(n_l + 11 + i, held[i], results[i]))
+
         small, early, late, sem_out, sem_z, sem_x, sem_s, sem_sz, sem_e, sem_l = take(10)
         rs_bufs = [take(4) for _ in range(n_groups + 1 + CHUNKS)]
         dn_bufs = [take(3) for _ in range(CHUNKS)]
@@ -354,6 +362,8 @@
             lc.append((dst, k))
             k += 1
         late[12] = jnp.zeros((16, 128), F32)
+        for cp in cv:
+            cp.wait()
         for i, r in enumerate(vec_in):
             late[12, i : i + 1, 0 : r.shape[0]] = r[...].astype(F32).reshape(1, r.shape[0])
         up_row = lax.broadcasted_iota(jnp.int32, (16, 128), 0) == UPB
@@ -483,6 +493,8 @@
         ok = jnp.logical_or(jnp.logical_and(kk < len_ref[r], down <= across), kk == qq)
         bias[r] = jnp.where(ok, 0.0, MASKED)
 
+    for cp in cl:
+        cp.wait()
     rows_loop(masks)
     sg[...] = jnp.zeros_like(sg)
     cx.wait()
@@ -580,6 +592,14 @@
     if not comm:
         lc[n_groups + 1].wait()
 
+    def grads(i, j):
+        cut = pl.ds(pl.multiple_of(i * (fc // 2), fc // 2), fc // 2)
+        g = tn(act[j * tokens : (j + 1) * tokens, cut], gv[...])
+        g_dn[j, pl.ds(2 * i, 2)] = g.astype(BF).reshape(2, *g_dn.shape[2:])
+        cut = pl.ds(pl.multiple_of(i * (D // 2), D // 2), D // 2)
+        g = nn(h2t[cut], dpre_s[(j % 2) * tokens : (j % 2 + 1) * tokens])
+        g_up[j][pl.ds(2 * i, 2)] = g.astype(BF).reshape(2, *g_up[j].shape[1:])
+
     for j in range(CHUNKS):
         if not comm:
             lc[n_groups + 2 + j].wait()
@@ -602,22 +622,8 @@
             back = nt(dl, wu)
             dh2[t] = back if j == 0 else dh2[t] + back
 
-        def grads(i, j=j - 1):
-            cut = pl.ds(pl.multiple_of(i * (fc // 2), fc // 2), fc // 2)
-            g = tn(act[j * tokens : (j + 1) * tokens, cut], gv[...])
-            g_dn[j, pl.ds(2 * i, 2)] = g.astype(BF).reshape(2, *g_dn.shape[2:])
-            cut = pl.ds(pl.multiple_of(i * (D // 2), D // 2), D // 2)
-            g = nn(h2t[cut], dpre_s[(j % 2) * tokens : (j % 2 + 1) * tokens])
-            g_up[j][pl.ds(2 * i, 2)] = g.astype(BF).reshape(2, *g_up[j].shape[1:])
-
-        rows_loop(feed, t_.feed[j], unroll=2, also=grads if j else None)
+        rows_loop(feed, t_.feed[j], unroll=2, also=functools.partial(grads, j=j - 1) if j else None)
         now(t_.fed[j])
-    j = CHUNKS - 1
-    now(t_.gdn)
-    g_dn[j] = tn(act[j * tokens : (j + 1) * tokens], gv[...]).astype(BF).reshape(g_dn.shape[1:])
-    now(t_.gup)
-    g_up[j][...] = nn(h2t[...], dpre_s[(j % 2) * tokens : (j % 2 + 1) * tokens]).astype(BF).reshape(g_up[j].shape)
-
     def second_back(r):
         t = tok(r)
         g2 = dh2[t]
@@ -631,9 +637,13 @@
         add(OB, col(dx))
         da[t] = dx.astype(BF)
 
-    rows_loop(second_back, t_.second_back, unroll=2)
-    now(t_.gwout)
-    g_wout[...] = tn(mixed[...], da[...]).astype(BF).reshape(g_wout.shape)
+    rows_loop(second_back, t_.second_back, unroll=2, also=functools.partial(grads, j=CHUNKS - 1))
+    now(t_.after)
+
+    def grad_out(i):
+        cut = pl.ds(pl.multiple_of(i * (D // 2), D // 2), D // 2)
+        g_wout[pl.ds(2 * i, 2)] = tn(mixed[:, cut], da[...]).astype(BF).reshape(2, *g_wout.shape[1:])
+
 
     for j in reversed(range(n_groups)):
         off, w = GROUPS[j]
@@ -666,7 +676,7 @@
                 dproj[j][t, pl.ds(w + p * 128, 128)] = dk.astype(BF)
                 dproj[j][t, pl.ds(2 * w + p * 128, 128)] = dv.astype(BF)
 
-        rows_loop(back, t_.back[j], unroll=2)
+        rows_loop(back, t_.back[j], unroll=2, also=grad_out if j == n_groups - 1 else None)
         now(t_.gqkv[j])
         g_qkv[j][...] = nn(h1t[...], dproj[j][...]).astype(BF).reshape(g_qkv[j].shape)
 
@@ -691,6 +701,8 @@
     co = start(0, outv, out_hbm)
     now(t_.tail)
     if comm:
+        for i in range(6):
+            hand(i)
         for k in range(4):
             room = me.bytes[id(sem_out), k] // (D * 2)
             wait_for((act, (pl.ds(0, room),)), (sem_out, (k,)))
@@ -699,6 +711,8 @@
         wait_for((small, (ALL, FOUR, 0)), (sem_out, (6,)))
         te.finish()
         tl.finish()
+        for cp in given_back:
+            cp.wait()
     else:
         sg_o[...] = sg[...]
         out_c = [start(2 + i, b, o) for i, (b, o) in enumerate(zip(g_qkv + [g_wout, g_dn] + g_up, g_out))]
@@ -716,15 +730,14 @@
     pieces = [blk(D // 32, 3 * w) for _, w in GROUPS] + [blk(D // 32, D), blk(ff // 32, D)] + [blk(D // 32, fc)] * CHUNKS
     any_ = pl.BlockSpec(memory_space=pl.ANY)
     vm = pl.BlockSpec(memory_space=pltpu.VMEM)
-    smem = pl.BlockSpec(memory_space=pltpu.SMEM)
-    in_specs = [any_, any_, smem, vm] + [vm] * (9 if comm else 1)
+    in_specs = [any_] * (4 + 9 if comm else 4) + [vm] * (0 if comm else 1)
     out_shape = [jax.ShapeDtypeStruct((tokens, D), BF), jax.ShapeDtypeStruct((tokens, D), F32)]
     out_specs = [any_, any_]
     if comm:
         in_specs += [any_] * 4
         out_shape += [jax.ShapeDtypeStruct(s, F32) for s in (
             (D // 32, 3 * D), (D // 32, D), (D // 32, ff), (ff // 32, D), (8, 128), (1, 128))]
-        out_specs += [vm] * 6
+        out_specs += [any_] * 6
     else:
         in_specs += [any_] * len(pieces) + [vm]
         out_shape += [jax.ShapeDtypeStruct(s, BF) for s in pieces] + [jax.ShapeDtypeStruct((16, D), F32)]
@@ -735,12 +748,14 @@
         V((rows, D // 128, 2 * slots, slots), BF), V((tokens, D), BF), V((tokens, D), F32), V((tokens, 128), F32),
         V((tokens, D), BF), V((D, tokens), BF), V((tokens, D), F32), V((tokens, D), F32), V((tokens, D), F32),
         V((CHUNKS * tokens, fc), BF), V((2 * tokens, fc), BF), V((tokens, D), BF), V((tokens, D), BF), V((24, D), F32), V((16, D), F32),
+        pltpu.SMEM((rows,), jnp.int32), V((rows, slots), jnp.int32),
     ]
     scratch += [V((tokens, 3 * w), BF) for _, w in GROUPS] * 2
     scratch += [V(s, BF) for s in pieces] * 2
-    scratch += [pltpu.SemaphoreType.DMA((2 + len(pieces),))]
+    scratch += [pltpu.SemaphoreType.DMA((2 + len(pieces) + 17,))]
     if comm:
         dma = pltpu.SemaphoreType.DMA
+        scratch += [V(o.shape, o.dtype) for o in out_shape[2:]] + [V(a.shape, a.dtype) for a in operands[4:13]]
         n_xy = n_groups + 1 + 2 * CHUNKS
         n_z = len(pieces) + 1
         scratch += [V(blk(16, 128), BF), V((14, 32, 128), F32), V((13, 16, 128), F32)]

time: 91.8 us -> 89.8 us (0.978)
  Pallas kernels: 90.7 us -> 88.7 us
    pallas_call x1, Pallas kernels: 86.5 us -> 84.5 us  [run_layer(): pl.pallas_call(functools.partial(layer, comm, rows, slots, ff), out_shape...]
where the time goes in v4:
time: 89.8 us; the launch traced here: 89.6 us
  Pallas kernels  88.7 us (99%)
    pallas_call x1, Pallas kernels, run_layer(): pl.pallas_call(functools.partial(layer, comm, rows, slots, ff), out_shape...  84.5 us
    pallas_call x1, Pallas kernels, run_deliver(): pl.pallas_call(functools.partial(deliver, n), out_shape=[jax.ShapeDtypeSt...  4.26 us

profile of v4, /device:TPU:0, one launch (start us, length us, event | category | flops | bytes accessed | tf_op | source)
XLA Modules:
  0.0 89.6 jit_solution(16528172883831554739)
XLA Ops:
  0.7 84.5 %shard_map.280 = (bf16[1024,512]{1,0:T(8,128)(2,1)}, f32[1024,512]{1,0:T(8,128)}, f32[16,1536]{1,0:T(8,128)}, f32[16,512]{1,0:T(8,128)}, f32[16,2048]{1,0:T(8,12...) custom-call(bf16[1024,512]{1,0:T(8,128)(2,1)} %bitcast.5, bf16[1024,512]{1,0:T(8,128)(2,1)} %bitcast.6, ...), custom_call_target="tpu_custom_call" | custom-call | flops 22000001024 | bytes 6291456 | tf_op jit(solution)/shard_map/pallas_call | solution.py:774
  85.1 4.3 %shard_map.281 = (bf16[1024,512]{1,0:T(8,128)(2,1)}, f32[1024,512]{1,0:T(8,128)}, f32[16,1536]{1,0:T(8,128)}, f32[16,512]{1,0:T(8,128)}, f32[16,2048]{1,0:T(8,12...) custom-call(bf16[1024,512]{1,0:T(8,128)(2,1)} %get-tuple-element.38., ...), custom_call_target="tpu_custom_call" | custom-call | tf_op jit(solution)/shard_map/pallas_call | solution.py:810
